TPU v7x, 32 devices: a whole 2x2x4 slice. The times are simulated.
32 devices in a mesh: gx: 4 (over y, x), gy: 8 (over z, core).
Axes of the slice: x: 2, y: 2, z: 4, core: 2. Of those that a mesh axis runs over, the one named last changes fastest.
Arguments:
- hidden: bfloat16 [64, 2, 16384], P('gy', None, 'gx'), may hold values from -6 to 6
- norm_gain: bfloat16 [16384], P('gx'), may hold values from 0.5 to 1.5
- w_query: bfloat16 [16384, 16384], P('gx', 'gy'), may hold values from -0.046875 to 0.046875
- w_keyval: bfloat16 [2, 16384, 1024], P(None, 'gx', 'gy'), may hold values from -0.046875 to 0.046875
- w_out: bfloat16 [16384, 16384], P('gy', 'gx'), may hold values from -0.046875 to 0.046875
- cache_keys: bfloat16 [64, 1024, 1024], P(('gx', 'gy')), may hold values from -80 to 80, as said below
- cache_values: bfloat16 [64, 1024, 1024], P(('gx', 'gy')), may hold values from -16 to 16
- cache_lengths: int32 [64], P(('gx', 'gy')), may hold values from 1 to 1024, as said below
- positions: int32 [64], P(('gx', 'gy')), may hold values from 1 to 5119, as said below
Outputs:
- attn_branch: bfloat16 [64, 2, 16384], P('gy', None, 'gx')
- new_keyvals: bfloat16 [2, 64, 2, 1024], P(None, ('gx', 'gy'))
Inputs may be any that keep to these rules, and one draw needn't show every extreme that they name: `cache_keys`: cached keys already carry their rotation. `cache_lengths`: some row has exactly 1024 valid slots and some row exactly 1. `positions`: each row's position is at least its cache length.
All inputs are finite; a program needn't handle non-finite values.
Results may differ from a plain program's by a relative error of at most 0.008.
The roundings to bfloat16 on the way count: a program that leaves them out, or rounds other values in their place, can miss the bound.
Values may be sent and summed in bfloat16 or wider, within the bound.
A program may use at most 128 MiB of HBM per device.

v0:
```python
import math

import jax
import jax.numpy as jnp
from jax import lax
from jax.sharding import PartitionSpec as P

D = 16384
HQ = 128
KVH = 8
HD = 128


norm_epsilon = 1e-05


def rope_rates():
    index = jnp.arange(HD // 2, dtype=jnp.float32)
    rates = 1.0 / jnp.power(500000.0, 2.0 * index / HD)
    wavelength = 2.0 * math.pi / rates
    smooth = (8192.0 / wavelength - 1.0) / 3.0
    blended = (1.0 - smooth) * rates / 8.0 + smooth * rates
    return jnp.where(
        wavelength > 8192.0, rates / 8.0, jnp.where(wavelength < 2048.0, rates, blended)
    )


def rotate(vectors, places):
    angles = places[..., None, None] * rope_rates()
    half_size = vectors.shape[-1] // 2
    first_half = vectors[..., :half_size]
    second_half = vectors[..., half_size:]
    cosine = jnp.cos(angles)
    sine = jnp.sin(angles)
    return jnp.concatenate(
        [first_half * cosine - second_half * sine, second_half * cosine + first_half * sine],
        axis=-1,
    )


def attend(queries, fresh_keys, fresh_values, cached_keys, cached_values, lengths):
    rows, steps = (queries.shape[0], queries.shape[1])
    slots = cached_keys.shape[1]
    grouped = queries.reshape(rows, steps, KVH, HQ // KVH, HD)
    old_keys = cached_keys.reshape(rows, slots, KVH, HD)
    old_values = cached_values.reshape(rows, slots, KVH, HD)
    score_scale = HD ** (-0.5)
    cached = (
        jnp.einsum("bskgd,btkd->bskgt", grouped, old_keys, preferred_element_type=jnp.float32)
        * score_scale
    )
    fresh = (
        jnp.einsum("bskgd,brkd->bskgr", grouped, fresh_keys, preferred_element_type=jnp.float32)
        * score_scale
    )
    slot_valid = jnp.arange(slots)[None, :] < lengths[:, None]
    step_valid = jnp.arange(steps)[None, :] <= jnp.arange(steps)[:, None]
    cached = jnp.where(slot_valid[:, None, None, None, :], cached, -1e30)
    fresh = jnp.where(step_valid[None, :, None, None, :], fresh, -1e30)
    highest = jnp.maximum(jnp.max(cached, axis=-1), jnp.max(fresh, axis=-1))[..., None]
    weights_old = jnp.exp(cached - highest)
    weights_new = jnp.exp(fresh - highest)
    denom = jnp.sum(weights_old, axis=-1) + jnp.sum(weights_new, axis=-1)
    mixed = jnp.einsum(
        "bskgt,btkd->bskgd",
        weights_old.astype(jnp.bfloat16),
        old_values,
        preferred_element_type=jnp.float32,
    )
    mixed = mixed + jnp.einsum(
        "bskgr,brkd->bskgd",
        weights_new.astype(jnp.bfloat16),
        fresh_values,
        preferred_element_type=jnp.float32,
    )
    return (mixed / denom[..., None]).astype(jnp.bfloat16).reshape(rows, steps, HQ * HD)


def on_device(
    hidden, norm_gain, w_query, w_keyval, w_out, cache_keys, cache_values, cache_lengths, positions
):
    steps = hidden.shape[1]
    features = hidden.astype(jnp.float32)
    squares = jnp.sum(features * features, axis=-1)
    square_sums = lax.psum(squares, "gx")
    inverse = lax.rsqrt(square_sums / D + norm_epsilon)
    normed = (features * inverse[..., None] * norm_gain.astype(jnp.float32)).astype(jnp.bfloat16)
    shard_rows = lax.all_gather(normed, "gy", axis=0, tiled=True)
    flattened = shard_rows.reshape(-1, shard_rows.shape[2])
    products = [
        jnp.dot(flattened, w_query, preferred_element_type=jnp.float32),
        jnp.dot(flattened, w_keyval[0], preferred_element_type=jnp.float32),
        jnp.dot(flattened, w_keyval[1], preferred_element_type=jnp.float32),
    ]
    partial_sums = jnp.concatenate(products, axis=-1).reshape(shard_rows.shape[0], steps, -1)
    width_parts = lax.axis_size("gx")
    head_parts = lax.axis_size("gy")
    block_rows = partial_sums.shape[0] // width_parts
    summed = lax.psum(partial_sums, "gx")
    summed = lax.dynamic_slice_in_dim(summed, lax.axis_index("gx") * block_rows, block_rows, 0)
    own_rows = summed.astype(jnp.bfloat16)
    arrived = lax.all_to_all(own_rows, "gy", split_axis=0, concat_axis=2, tiled=True)
    local_rows = arrived.shape[0]
    pieces = arrived.reshape(local_rows, steps, head_parts, -1)
    query_cols = w_query.shape[1]
    keyval_cols = w_keyval.shape[2]
    queries = pieces[..., :query_cols].reshape(local_rows, steps, HQ, HD)
    fresh_keys = pieces[..., query_cols : query_cols + keyval_cols].reshape(
        local_rows, steps, KVH, HD
    )
    fresh_values = pieces[..., query_cols + keyval_cols :].reshape(local_rows, steps, KVH, HD)
    places = positions.astype(jnp.float32)[:, None] + jnp.arange(steps, dtype=jnp.float32)[None, :]
    turned_queries = rotate(queries.astype(jnp.float32), places).astype(jnp.bfloat16)
    turned_keys = rotate(fresh_keys.astype(jnp.float32), places).astype(jnp.bfloat16)
    new_keyvals = jnp.stack(
        [
            turned_keys.reshape(local_rows, steps, KVH * HD),
            fresh_values.reshape(local_rows, steps, KVH * HD),
        ]
    )
    attended = attend(
        turned_queries, turned_keys, fresh_values, cache_keys, cache_values, cache_lengths
    )
    returned = lax.all_to_all(attended, "gy", split_axis=2, concat_axis=0, tiled=True)
    rows_all = lax.all_gather(returned, "gx", axis=0, tiled=True)
    head_cols = rows_all.shape[2]
    all_rows = rows_all.shape[0]
    out_rows_here = all_rows // head_parts
    product = jnp.dot(
        rows_all.reshape(lax.axis_size("gy") * out_rows_here * steps, head_cols),
        w_out,
        preferred_element_type=jnp.float32,
    )
    branch = lax.psum_scatter(
        product.reshape(lax.axis_size("gy") * out_rows_here, steps, -1),
        "gy",
        scatter_dimension=0,
        tiled=True,
    )
    return (branch.astype(jnp.bfloat16), new_keyvals)


def solution(mesh):
    return jax.shard_map(
        on_device,
        mesh=mesh,
        in_specs=(
            P("gy", None, "gx"),
            P("gx"),
            P("gx", "gy"),
            P(None, "gx", "gy"),
            P("gy", "gx"),
            P(("gx", "gy"), None, None),
            P(("gx", "gy"), None, None),
            P(("gx", "gy")),
            P(("gx", "gy")),
        ),
        out_specs=(P("gy", None, "gx"), P(None, ("gx", "gy"), None, None)),
        check_vma=False,
    )
```

profile of v0, /device:TPU:0, one launch (start us, length us, event | category | flops | bytes accessed | tf_op | source)
XLA Modules:
  0.0 247.0 jit_solution(2336805116317348478)
XLA Ops:
  8.3 11.3 %psum.14 = f32[8,2]{1,0:T(8,128)S(1)} all-reduce(f32[8,2]{1,0:T(8,128)S(1)} %fusion.28), channel_id=1, replica_groups=mesh['gx'=4,'gy'=8] {'gx'}, use_global_device_ids=true, to_apply=%region_1.0 | all-reduce | flops 16 | bytes 128 | tf_op jit(solution)/shard_map/psum | solution.py:85
  20.4 1.8 fusion.30
  22.8 5.4 %copy.72 = bf16[256,8,8,128]{3,2,1,0:T(8,128)(2,1)} copy(bf16[256,8,8,128]{3,1,2,0:T(8,128)(2,1)} %bitcast.81) | data formatting | bytes 8388608
  28.3 3.1 %copy.73 = bf16[256,8,8,128]{3,2,1,0:T(8,128)(2,1)} copy(bf16[256,8,8,128]{3,1,2,0:T(8,128)(2,1)S(1)} %bitcast.82) | data formatting | bytes 8388608
  31.5 4.5 %bitcast_bitcast_fusion.1 = bf16[2,1024,8,128,1]{3,2,1,0,4:T(8,128)(2,1)} fusion(bf16[2,1024,8,128]{3,2,1,0:T(8,128)(2,1)} %bitcast.80), kind=kLoop, calls=%fused_computation.3 | loop fusion | bytes 8388608 | tf_op jit(solution)/shard_map/reshape | solution.py:45
  36.0 2.2 bitcast_bitcast_fusion
  38.3 5.4 %all-gather.2.cloned.1.call-done = bf16[64,2,4096]{2,1,0:T(2,128)(2,1)} async-done(((bf16[8,2,4096]{2,1,0:T(2,128)(2,1)}), bf16[64,2,4096]{2,1,0:T(2,128)(2,1)}) %all-gather.2.cloned.1.call-update) | async-done | bytes 1048592 | tf_op jit(solution)/shard_map/all_gather | solution.py:88
  43.7 1.5 reshape.138
  45.2 1.6 fusion.18
  46.8 1.6 fusion.20
  48.5 8.1 %fusion.43 = f32[128,2048]{1,0:T(8,128)S(1)} fusion(bf16[128,4096]{1,0:T(8,128)(2,1)S(1)} %reshape.138, bf16[4096,2048]{1,0:T(8,128)(2,1)} %param.11), kind=kOutput, calls=%fused_computation.70 | convolution fusion | flops 2147483648 | bytes 18874368 | tf_op jit(solution)/shard_map/dot_general | solution.py:91
  57.4 46.4 %all-reduce.1 = bf16[64,2,2304]{2,1,0:T(2,128)(2,1)S(1)} all-reduce(f32[64,2,2304]{2,1,0:T(2,128)S(1)} %reshape.139), channel_id=1, replica_groups=mesh['gx'=4,'gy'=8] {'gx'}, use_global_device_ids=true, to_apply=%region_2.0 | all-reduce | flops 294912 | bytes 1769472 | tf_op jit(solution)/shard_map/psum | solution.py:99
  104.6 3.4 %all-to-all-start = ((bf16[16,2,2304]{2,1,0:T(2,128)(2,1)}), bf16[16,2,2304]{2,1,0:T(2,128)(2,1)S(1)}, u32[]{:S(2)}, u32[]{:S(2)}) async-start(bf16[16,2,2304]{2,1,0:T(2,128)(2,1)} %dynamic-slice_convert_fusion), calls=%async_computation | async-start | bytes 294912 | tf_op jit(solution)/shard_map/all_to_all | solution.py:102
  108.4 6.6 %all-to-all-done = bf16[16,2,2304]{2,1,0:T(2,128)(2,1)S(1)} async-done(((bf16[16,2,2304]{2,1,0:T(2,128)(2,1)}), bf16[16,2,2304]{2,1,0:T(2,128)(2,1)S(1)}, u32[]{:S(2)}, u32[]{:S(2)}) %all-to-all-start) | async-done | bytes 147488 | tf_op jit(solution)/shard_map/all_to_all | solution.py:102
  116.0 4.0 %bitcast_reduce_fusion = (f32[2,2,8,16]{3,1,2,0:T(2,128)S(1)}, f32[2,8,2,16,1024]{4,3,2,1,0:T(8,128)S(1)}) fusion(pred[2,1024]{1,0:T(4,128)(4,1)S(1)} %iota_compare_fusion, bf16[2,1024,8,128,1]{3,2,1,0,4:T(8,128)(2,1)} %bitcast_bitcast_fusion.1, bf16[2,2,8,16,128]{4,3,2,1,0:T(8,128)(2,1)S(1)} %pad_maximum_fusion.1), kind=kOutput, calls=%fused_computation.9 | convolution fusion | flops 135790080 | bytes 6426624 | tf_op jit(solution)/shard_map/bskgd,btkd->bskgt/dot_general | solution.py:49
  120.7 1.6 fusion.9
  122.6 9.4 %copy.69 = bf16[2,2,8,16,128]{1,0,4,3,2:T(2,128)(2,1)} copy(bf16[2,2,8,16,128]{4,3,1,2,0:T(8,128)(2,1)S(1)} %fusion.14) | data formatting | bytes 262144 | tf_op jit(solution)/shard_map/reshape | solution.py:76
  132.0 13.1 %reshape.149 = bf16[8,2,4096]{2,1,0:T(2,128)(2,1)S(1)} reshape(bf16[16384,2,2]{2,1,0:T(2,128)(2,1)} %bitcast.77) | data formatting | bytes 262144
  145.1 9.4 %all_to_all.33 = bf16[8,2,4096]{2,1,0:T(2,128)(2,1)S(1)} all-to-all(bf16[8,2,4096]{2,1,0:T(2,128)(2,1)S(1)} %reshape.149), channel_id=1, replica_groups=mesh['gx'=4,'gy'=8] {'gy'}, dimensions={0} | all-to-all | bytes 262144 | tf_op jit(solution)/shard_map/all_to_all | solution.py:124
  154.5 19.1 %reshape.150 = bf16[16384,2,2]{2,1,0:T(2,128)(2,1)} reshape(bf16[8,2,4096]{2,1,0:T(2,128)(2,1)S(1)} %all_to_all.33) | data formatting | bytes 262144
  173.5 11.9 %copy.70 = bf16[2,2,8,2048]{3,2,1,0:T(8,128)(2,1)S(1)} copy(bf16[2,2,8,2048]{1,0,3,2:T(2,128)(2,1)} %bitcast.78) | data formatting | bytes 262144 | tf_op jit(solution)/shard_map/all_to_all | solution.py:124
  185.6 9.3 %all_gather.7 = bf16[64,2,2048]{2,0,1:T(8,128)(2,1)S(1)} all-gather(bf16[16,2,2048]{2,0,1:T(8,128)(2,1)S(1)} %all_to_all.30), channel_id=1, replica_groups=mesh['gx'=4,'gy'=8] {'gx'}, dimensions={0}, use_global_device_ids=true | all-gather | bytes 655360 | tf_op jit(solution)/shard_map/all_gather | solution.py:125
  194.9 9.5 %fusion = f32[64,2,4096]{2,0,1:T(8,128)} fusion(bf16[64,2,2048]{2,0,1:T(8,128)(2,1)S(1)} %all_gather.7, bf16[2048,4096]{1,0:T(8,128)(2,1)} %param.13), kind=kOutput, calls=%fused_computation | convolution fusion | flops 2147483648 | bytes 19398656 | tf_op jit(solution)/shard_map/dot_general | solution.py:129
  205.1 33.3 %reduce-scatter.2.cloned.1.call-done = f32[8,2,4096]{2,0,1:T(8,128)} async-done(((f32[64,2,4096]{2,0,1:T(8,128)}), f32[8,2,4096]{2,0,1:T(8,128)}) %reduce-scatter.2.cloned.1.call-update) | async-done | bytes 262160 | tf_op jit(solution)/shard_map/reduce_scatter | solution.py:134
  (46 shorter events, 9.2 us)
Async XLA Ops:
  7.2 36.6 %all-gather.2.cloned.1.call-start = ((), (), s32[]{:S(2)}) async-start(), calls=%async_computation.3 | async-start | bytes 1179648 | tf_op jit(solution)/shard_map/all_gather | solution.py:88
  22.8 5.4 %copy-start.1 = (bf16[2,1024,1024]{2,1,0:T(8,128)(2,1)S(1)}, bf16[2,1024,1024]{2,1,0:T(8,128)(2,1)}, u32[]{:S(2)}) copy-start(bf16[2,1024,1024]{2,1,0:T(8,128)(2,1)} %param.15) | copy-start | bytes 12582916
  28.3 3.1 %copy-start.3 = (s32[2]{0:T(128)S(1)}, s32[2]{0:T(128)}, u32[]{:S(2)}) copy-start(s32[2]{0:T(128)} %param.16) | copy-start | bytes 28
  31.5 4.5 %copy-start = (bf16[256,8,8,128]{3,2,1,0:T(8,128)(2,1)S(1)}, bf16[256,8,8,128]{3,2,1,0:T(8,128)(2,1)}, u32[]{:S(2)}) copy-start(bf16[256,8,8,128]{3,2,1,0:T(8,128)(2,1)} %copy.73) | copy-start | bytes 12582916
  104.6 10.3 %all-to-all-start = ((bf16[16,2,2304]{2,1,0:T(2,128)(2,1)}), bf16[16,2,2304]{2,1,0:T(2,128)(2,1)S(1)}, u32[]{:S(2)}, u32[]{:S(2)}) async-start(bf16[16,2,2304]{2,1,0:T(2,128)(2,1)} %dynamic-slice_convert_fusion), calls=%async_computation | async-start | bytes 294912 | tf_op jit(solution)/shard_map/all_to_all | solution.py:102
  108.0 130.4 %reduce-scatter.2.cloned.1.call-start = ((), (), s32[]{:S(2)}) async-start(), calls=%async_computation.4 | async-start | bytes 2359296 | tf_op jit(solution)/shard_map/reduce_scatter | solution.py:134
  115.9 4.7 %copy-start.2 = (bf16[2,1024,8,128,1]{3,2,1,0,4:T(8,128)(2,1)S(1)}, bf16[2,1024,8,128,1]{3,2,1,0,4:T(8,128)(2,1)}, u32[]{:S(2)}) copy-start(bf16[2,1024,8,128,1]{3,2,1,0,4:T(8,128)(2,1)} %bitcast_bitcast_fusion) | copy-start | bytes 12582916
Sparse Core Ops, SparseCore 0:
  22.3 21.3 all-gather.1
  204.5 33.8 reduce-scatter.1
where the time goes:
time: 248 us; the launch traced here: 247 us
  blocking collectives  76.4 us (31%)
  local copies, waits for them, and re-layouts  72.8 us (29%)
  waiting for transfers between devices  45.3 us (18%)
  matrix products  27.2 us (11%)
  between operations  14.2 us (6%)
  other arithmetic  7.43 us (3%)
  starting transfers between devices  3.64 us (1%)
    psum x1, blocking collectives, on_device(): summed = lax.psum(partial_sums, 'gx')  46.4 us
    unnamed x13, local copies, waits for them, and re-layouts  41.5 us
    reduce_scatter x1, waiting for transfers between devices, on_device(): lax.psum_scatter(product.reshape(lax.axis_size('gy') * out_rows_here, ste...  33.3 us
    all_to_all x3, local copies, waits for them, and re-layouts, on_device(): lax.all_to_all(attended, 'gy', split_axis=2, concat_axis=0, tiled=True)  12.1 us
    psum x1, blocking collectives, on_device(): square_sums = lax.psum(squares, 'gx')  11.3 us
    dot_general x1, matrix products, on_device(): jnp.dot(rows_all.reshape(lax.axis_size('gy') * out_rows_here * steps, hea...  9.5 us
    reshape x1, local copies, waits for them, and re-layouts, attend(): (mixed / denom[..., None]).astype(jnp.bfloat16)  9.4 us
    all_to_all x1, blocking collectives, on_device(): lax.all_to_all(attended, 'gy', split_axis=2, concat_axis=0, tiled=True)  9.37 us
  transfers between devices with their start and end apart: 3, of which 3 were waited for; matrix products, arithmetic and copies ran while one was open for 7% of the time, Pallas kernels for 0%

commit v1 on v0

--- a/solution.py
+++ b/solution.py
@@ -1,14 +1,18 @@
+import functools
 import math
 
 import jax
 import jax.numpy as jnp
 from jax import lax
+from jax.experimental import pallas as pl
+from jax.experimental.pallas import tpu as pltpu
 from jax.sharding import PartitionSpec as P
 
 D = 16384
 HQ = 128
 KVH = 8
 HD = 128
+STEPS = 2
 
 
 norm_epsilon = 1e-05
@@ -76,7 +80,7 @@
     return (mixed / denom[..., None]).astype(jnp.bfloat16).reshape(rows, steps, HQ * HD)
 
 
-def on_device(
+def plain(
     hidden, norm_gain, w_query, w_keyval, w_out, cache_keys, cache_values, cache_lengths, positions
 ):
     steps = hidden.shape[1]
@@ -140,6 +144,492 @@
     return (branch.astype(jnp.bfloat16), new_keyvals)
 
 
+def peer_id(axis, index):
+    return {axis: index}
+
+
+def remote(src, dst, send_sem, recv_sem, axis, index):
+    return pltpu.make_async_remote_copy(
+        src_ref=src,
+        dst_ref=dst,
+        send_sem=send_sem,
+        recv_sem=recv_sem,
+        device_id=peer_id(axis, index),
+        device_id_type=pl.DeviceIdType.MESH,
+    )
+
+
+def greet(x, y, nx, ny):
+    barrier = pltpu.get_barrier_semaphore()
+    for d in range(1, nx):
+        pl.semaphore_signal(
+            barrier, inc=1, device_id=peer_id("gx", lax.rem(x + d, nx)),
+            device_id_type=pl.DeviceIdType.MESH,
+        )
+    for d in range(1, ny):
+        pl.semaphore_signal(
+            barrier, inc=1, device_id=peer_id("gy", lax.rem(y + d, ny)),
+            device_id_type=pl.DeviceIdType.MESH,
+        )
+    pl.semaphore_wait(barrier, nx - 1 + ny - 1)
+
+
+def project_kernel(
+    nx, ny, x_ref, gain_ref, wq_hbm, wkv_hbm, out_ref,
+    wq, wkv, xbuf, sqbuf, parts, rbuf, qbuf, kvbuf, sendbuf, landed,
+    wq_sem, wkv_sem, sq_s, sq_r, g_s, g_r, rs_s, rs_r, a_s, a_r,
+):
+    x = lax.axis_index("gx")
+    y = lax.axis_index("gy")
+    nz = ny // 2
+    z = y // 2
+    c = lax.rem(y, 2)
+    nblocks = wq.shape[0]
+    bc = wq.shape[2]
+    head = wkv.shape[2]
+    chunk = rbuf.shape[2]
+
+    def load_q(j):
+        cols = pl.ds(j * bc, bc) if isinstance(j, int) else pl.ds(pl.multiple_of(j * bc, bc), bc)
+        return pltpu.make_async_copy(wq_hbm.at[:, cols], wq.at[j], wq_sem.at[j])
+
+    def load_kv():
+        return pltpu.make_async_copy(wkv_hbm, wkv, wkv_sem)
+
+    load_kv().start()
+    for j in range(nblocks):
+        load_q(j).start()
+
+    features = x_ref[...].astype(jnp.float32)
+    squares = jnp.sum(features * features, axis=-1, keepdims=True)
+    sqbuf[0] = jnp.broadcast_to(squares, sqbuf.shape[1:])
+    greet(x, y, nx, ny)
+    sq_copies = [
+        remote(sqbuf.at[0], sqbuf.at[d], sq_s.at[d - 1], sq_r.at[d - 1], "gx", lax.rem(x + d, nx))
+        for d in range(1, nx)
+    ]
+    for copy in sq_copies:
+        copy.start()
+    for copy in sq_copies:
+        copy.wait_recv()
+    total = sqbuf[0]
+    for d in range(1, nx):
+        total = total + sqbuf[d]
+    inverse = lax.rsqrt(total[:, :1] / D + norm_epsilon)
+    xbuf[y] = (features * inverse * gain_ref[...].astype(jnp.float32)).astype(jnp.bfloat16)
+
+    def hop(block, k):
+        dest = (y - 2, y + 2, y + 1 - 2 * c)[k]
+        return remote(xbuf.at[block], xbuf.at[block], g_s.at[block, k], g_r.at[block], "gy", dest)
+
+    @pl.when(z > 0)
+    def _():
+        hop(y, 0).start()
+
+    @pl.when(z < nz - 1)
+    def _():
+        hop(y, 1).start()
+
+    hop(y, 2).start()
+    for d in range(1, nz):
+
+        @pl.when(z - d >= 0)
+        def _():
+            block = y - 2 * d
+            hop(block, 2).wait_recv()
+
+            @pl.when(z < nz - 1)
+            def _():
+                hop(block, 1).start()
+
+            hop(block, 2).start()
+
+        @pl.when(z + d < nz)
+        def _():
+            block = y + 2 * d
+            hop(block, 2).wait_recv()
+
+            @pl.when(z > 0)
+            def _():
+                hop(block, 0).start()
+
+            hop(block, 2).start()
+
+    for zz in range(nz):
+        hop(2 * zz + 1 - c, 2).wait_recv()
+
+    def rs(j, d):
+        to = lax.rem(x + d, nx)
+        rows = pl.ds(pl.multiple_of(to * chunk, chunk), chunk)
+        return remote(
+            parts.at[j, rows, :], rbuf.at[d - 1, j], rs_s.at[d - 1, j], rs_r.at[d - 1, j], "gx", to
+        )
+
+    tokens = xbuf.shape[0] * xbuf.shape[1]
+    load_kv().wait()
+    for n in range(2):
+        parts[nblocks, :, n * head : (n + 1) * head] = jnp.dot(
+            xbuf[...].reshape(tokens, xbuf.shape[2]), wkv[n], preferred_element_type=jnp.float32
+        )
+    for d in range(1, nx):
+        rs(nblocks, d).start()
+
+    def block_step(j, carry):
+        load_q(j).wait()
+        parts[j] = jnp.dot(
+            xbuf[...].reshape(tokens, xbuf.shape[2]), wq[j], preferred_element_type=jnp.float32
+        )
+        for d in range(1, nx):
+            rs(j, d).start()
+        return carry
+
+    lax.fori_loop(0, nblocks, block_step, 0)
+
+    own = pl.ds(pl.multiple_of(x * chunk, chunk), chunk)
+    per_block = bc // head
+    heads = nblocks * per_block
+    kvbuf[...] = jnp.zeros_like(kvbuf)
+    for j in [nblocks] + list(range(nblocks)):
+        for d in range(1, nx):
+            rs(j, d).wait_recv()
+        summed = parts[j, own, :]
+        for d in range(1, nx):
+            summed = summed + rbuf[d - 1, j]
+        for i in range(per_block):
+            piece = summed[:, i * head : (i + 1) * head]
+            if j < nblocks:
+                qbuf[pl.ds(j * per_block + i, chunk, stride=heads), :] = piece
+            else:
+                kvbuf[pl.ds(i, chunk, stride=4), :] = piece
+    local = chunk // ny
+    sendbuf[:, : local * heads, :] = (
+        qbuf[...].astype(jnp.bfloat16).reshape(ny, local * heads, head)
+    )
+    sendbuf[:, local * heads :, :] = kvbuf[...].astype(jnp.bfloat16).reshape(ny, local * 4, head)
+
+    def a2a(d):
+        to = lax.rem(y + d, ny)
+        return remote(sendbuf.at[to], landed.at[y], a_s.at[d - 1], a_r.at[d - 1], "gy", to)
+
+    for d in range(1, ny):
+        a2a(d).start()
+    landed[y] = sendbuf[y]
+    for d in range(1, ny):
+        a2a(d).wait_recv()
+    out_ref[...] = landed[...]
+
+    for copy in sq_copies:
+        copy.wait_send()
+    for zz in range(nz):
+        block = 2 * zz + c
+        hop(block, 2).wait_send()
+
+        @pl.when((zz >= z) & (z > 0))
+        def _():
+            hop(block, 0).wait_send()
+
+        @pl.when((zz <= z) & (z < nz - 1))
+        def _():
+            hop(block, 1).wait_send()
+
+    def rs_done(j, carry):
+        for d in range(1, nx):
+            rs(j, d).wait_send()
+        return carry
+
+    lax.fori_loop(0, nblocks + 1, rs_done, 0)
+    for d in range(1, ny):
+        a2a(d).wait_send()
+
+
+def attend_kernel(len_ref, x_ref, cos_ref, sin_ref, key_ref, val_ref, out_ref, kv_ref):
+    rows = key_ref.shape[0]
+    slots = key_ref.shape[1]
+    head = key_ref.shape[2]
+    steps = STEPS
+    group = (x_ref.shape[1] // rows - 4 * steps) // steps
+    nq = steps * group
+    scale = HD ** (-0.5)
+    raw = x_ref[0].astype(jnp.float32)
+    swapped = jnp.concatenate([raw[:, head // 2 :], raw[:, : head // 2]], axis=1)
+    turned = (raw * cos_ref[...] + swapped * sin_ref[...]).astype(jnp.bfloat16)
+    turned_f = turned.astype(jnp.float32)
+    col = lax.broadcasted_iota(jnp.int32, (nq, 4 * steps), 1)
+    step = lax.broadcasted_iota(jnp.int32, (nq, 4 * steps), 0) // group
+    keep_new = (col % 4 == 0) & (col // 4 <= step)
+    slot = lax.broadcasted_iota(jnp.int32, (nq, slots), 1)
+    keys_out, values_out = [], []
+    for b in range(rows):
+        q = turned[b * nq : (b + 1) * nq]
+        base = rows * nq + b * 4 * steps
+        kv_turned = turned_f[base : base + 4 * steps]
+        kv_raw = raw[base : base + 4 * steps]
+        old = lax.dot_general(
+            q, key_ref[b], (((1,), (1,)), ((), ())), preferred_element_type=jnp.float32
+        ) * scale
+        new = lax.dot_general(
+            q, kv_turned.astype(jnp.bfloat16), (((1,), (1,)), ((), ())),
+            preferred_element_type=jnp.float32,
+        ) * scale
+        old = jnp.where(slot < len_ref[b], old, -1e30)
+        new = jnp.where(keep_new, new, -1e30)
+        highest = jnp.maximum(
+            jnp.max(old, axis=-1, keepdims=True), jnp.max(new, axis=-1, keepdims=True)
+        )
+        old = jnp.exp(old - highest)
+        new = jnp.exp(new - highest)
+        denom = jnp.sum(old, axis=-1, keepdims=True) + jnp.sum(new, axis=-1, keepdims=True)
+        mixed = jnp.dot(old.astype(jnp.bfloat16), val_ref[b], preferred_element_type=jnp.float32)
+        new = new.astype(jnp.bfloat16).astype(jnp.float32)
+        for r in range(steps):
+            mixed = mixed + new[:, 4 * r : 4 * r + 1] * kv_raw[4 * r + 1 : 4 * r + 2]
+            keys_out.append(kv_turned[4 * r : 4 * r + 1])
+            values_out.append(kv_raw[4 * r + 1 : 4 * r + 2])
+        out_ref[0, b * nq : (b + 1) * nq] = (mixed / denom).astype(jnp.bfloat16)
+    kv_ref[...] = jnp.concatenate(keys_out + values_out, axis=0)
+
+
+def output_kernel(
+    nx, ny, att_ref, wo_hbm, out_ref,
+    wo, abuf, fbuf, lbuf, prod, sbuf, rbuf, chip, zsend, zland,
+    wo_sem, a_s, a_r, g_s, g_r, c_s, c_r, z_s, z_r,
+):
+    x = lax.axis_index("gx")
+    y = lax.axis_index("gy")
+    nz = ny // 2
+    z = y // 2
+    c = lax.rem(y, 2)
+    nblocks = wo.shape[0]
+    bc = wo.shape[2]
+
+    def load(j):
+        cols = pl.ds(j * bc, bc) if isinstance(j, int) else pl.ds(pl.multiple_of(j * bc, bc), bc)
+        return pltpu.make_async_copy(wo_hbm.at[:, cols], wo.at[j], wo_sem.at[j])
+
+    for j in range(nblocks):
+        load(j).start()
+    greet(x, y, nx, ny)
+
+    def a2a(d):
+        to = lax.rem(y + d, ny)
+        return remote(att_ref.at[to], abuf.at[y], a_s.at[d - 1], a_r.at[d - 1], "gy", to)
+
+    for d in range(1, ny):
+        a2a(d).start()
+    abuf[y] = att_ref[y]
+    for d in range(1, ny):
+        a2a(d).wait_recv()
+    head = abuf.shape[2]
+    chunk = lbuf.shape[1]
+    heads = lbuf.shape[2] // head
+    fbuf[...] = abuf[...].astype(jnp.float32).reshape(fbuf.shape)
+    for h in range(heads):
+        lbuf[x, :, h * head : (h + 1) * head] = fbuf[
+            pl.ds(h, chunk, stride=heads), :
+        ].astype(jnp.bfloat16)
+
+    def gather(d):
+        return remote(
+            lbuf.at[x], lbuf.at[x], g_s.at[d - 1], g_r.at[d - 1], "gx", lax.rem(x + d, nx)
+        )
+
+    for d in range(1, nx):
+        gather(d).start()
+    for d in range(1, nx):
+        gather(d).wait_recv()
+
+    def pair(j):
+        return remote(sbuf.at[j], rbuf.at[j], c_s.at[j], c_r.at[j], "gy", y + 1 - 2 * c)
+
+    def along(j, d):
+        to = lax.rem(z + d, nz)
+        return remote(
+            zsend.at[j, to], zland.at[d - 1, j], z_s.at[d - 1, j], z_r.at[d - 1, j], "gy", 2 * to + c
+        )
+
+    def pass_on(j):
+        pair(j).wait_recv()
+        chip[j] = prod[j, :, c] + rbuf[j].astype(jnp.float32)
+        zsend[j] = chip[j].astype(jnp.bfloat16)
+        for d in range(1, nz):
+            along(j, d).start()
+
+    def block_step(j, carry):
+        load(j).wait()
+        prod[j] = jnp.dot(
+            lbuf[...].reshape(nx * chunk, lbuf.shape[2]), wo[j], preferred_element_type=jnp.float32
+        ).reshape(prod.shape[1:])
+        sbuf[j] = prod[j, :, 1 - c].astype(jnp.bfloat16)
+        pair(j).start()
+
+        @pl.when(j > 0)
+        def _():
+            pass_on(j - 1)
+
+        return carry
+
+    lax.fori_loop(0, nblocks, block_step, 0)
+    pass_on(nblocks - 1)
+    for j in range(nblocks):
+        total = chip[j, z]
+        for d in range(1, nz):
+            along(j, d).wait_recv()
+            total = total + zland[d - 1, j].astype(jnp.float32)
+        out_ref[:, j * bc : (j + 1) * bc] = total.astype(jnp.bfloat16)
+
+    for d in range(1, ny):
+        a2a(d).wait_send()
+    for d in range(1, nx):
+        gather(d).wait_send()
+
+    def done(j, carry):
+        pair(j).wait_send()
+        for d in range(1, nz):
+            along(j, d).wait_send()
+        return carry
+
+    lax.fori_loop(0, nblocks, done, 0)
+
+
+def with_kernels(
+    hidden, norm_gain, w_query, w_keyval, w_out, cache_keys, cache_values, cache_lengths, positions
+):
+    nx = lax.axis_size("gx")
+    ny = lax.axis_size("gy")
+    nz = ny // 2
+    rows, steps, width = hidden.shape
+    mine = rows * steps
+    tokens = ny * mine
+    chunk = tokens // nx
+    local_rows = cache_keys.shape[0]
+    local = local_rows * steps
+    cols = w_query.shape[1]
+    heads = cols // HD
+    bc = 256
+    nq = cols // bc
+    packed = local * heads + local * 4
+    vmem = pl.BlockSpec(memory_space=pltpu.VMEM)
+    hbm = pl.BlockSpec(memory_space=pl.ANY)
+    dma = pltpu.SemaphoreType.DMA
+    arrived = pl.pallas_call(
+        functools.partial(project_kernel, nx, ny),
+        out_shape=jax.ShapeDtypeStruct((ny, packed, HD), jnp.bfloat16),
+        in_specs=[vmem, vmem, hbm, hbm],
+        out_specs=vmem,
+        scratch_shapes=[
+            pltpu.VMEM((nq, width, bc), jnp.bfloat16),
+            pltpu.VMEM(w_keyval.shape, jnp.bfloat16),
+            pltpu.VMEM((ny, mine, width), jnp.bfloat16),
+            pltpu.VMEM((nx, mine, 128), jnp.float32),
+            pltpu.VMEM((nq + 1, tokens, bc), jnp.float32),
+            pltpu.VMEM((nx - 1, nq + 1, chunk, bc), jnp.float32),
+            pltpu.VMEM((chunk * heads, HD), jnp.float32),
+            pltpu.VMEM((chunk * 4, HD), jnp.float32),
+            pltpu.VMEM((ny, packed, HD), jnp.bfloat16),
+            pltpu.VMEM((ny, packed, HD), jnp.bfloat16),
+            dma((nq,)),
+            dma(()),
+            dma((nx - 1,)),
+            dma((nx - 1,)),
+            dma((ny, 3)),
+            dma((ny,)),
+            dma((nx - 1, nq + 1)),
+            dma((nx - 1, nq + 1)),
+            dma((ny - 1,)),
+            dma((ny - 1,)),
+        ],
+        compiler_params=pltpu.CompilerParams(
+            collective_id=0, has_side_effects=True, vmem_limit_bytes=48 * 1024 * 1024
+        ),
+        name="project",
+    )(hidden.reshape(mine, width), norm_gain.reshape(1, width), w_query, w_keyval)
+
+    places = positions.astype(jnp.float32)[:, None] + jnp.arange(steps, dtype=jnp.float32)[None, :]
+    angles = places.reshape(local, 1) * rope_rates()[None, :]
+    cosine, sine = jnp.cos(angles), jnp.sin(angles)
+    cosine = jnp.concatenate([cosine, cosine], axis=-1)
+    sine = jnp.concatenate([-sine, sine], axis=-1)
+    spread = lambda table: jnp.concatenate(
+        [jnp.repeat(table, heads, axis=0), jnp.repeat(table, 4, axis=0)], axis=0
+    )
+    slots = cache_keys.shape[1]
+    attended, new = pl.pallas_call(
+        attend_kernel,
+        grid=(ny,),
+        out_shape=(
+            jax.ShapeDtypeStruct((ny, local * heads, HD), jnp.bfloat16),
+            jax.ShapeDtypeStruct((2 * local, KVH * HD), jnp.float32),
+        ),
+        in_specs=[
+            pl.BlockSpec(memory_space=pltpu.SMEM),
+            pl.BlockSpec((1, packed, HD), lambda g: (g, 0, 0)),
+            pl.BlockSpec((packed, HD), lambda g: (0, 0)),
+            pl.BlockSpec((packed, HD), lambda g: (0, 0)),
+            pl.BlockSpec((local_rows, slots, HD), lambda g: (0, 0, g)),
+            pl.BlockSpec((local_rows, slots, HD), lambda g: (0, 0, g)),
+        ],
+        out_specs=(
+            pl.BlockSpec((1, local * heads, HD), lambda g: (g, 0, 0)),
+            pl.BlockSpec((2 * local, HD), lambda g: (0, g)),
+        ),
+        compiler_params=pltpu.CompilerParams(vmem_limit_bytes=32 * 1024 * 1024),
+        name="attend",
+    )(cache_lengths, arrived, spread(cosine), spread(sine), cache_keys, cache_values)
+    new_keyvals = new.astype(jnp.bfloat16).reshape(2, local_rows, steps, KVH * HD)
+
+    oc = 512
+    no = w_out.shape[1] // oc
+    branch = pl.pallas_call(
+        functools.partial(output_kernel, nx, ny),
+        out_shape=jax.ShapeDtypeStruct((mine, w_out.shape[1]), jnp.bfloat16),
+        in_specs=[vmem, hbm],
+        out_specs=vmem,
+        scratch_shapes=[
+            pltpu.VMEM((no, cols, oc), jnp.bfloat16),
+            pltpu.VMEM((ny, local * heads, HD), jnp.bfloat16),
+            pltpu.VMEM((chunk * heads, HD), jnp.float32),
+            pltpu.VMEM((nx, chunk, cols), jnp.bfloat16),
+            pltpu.VMEM((no, nz, 2, mine, oc), jnp.float32),
+            pltpu.VMEM((no, nz, mine, oc), jnp.bfloat16),
+            pltpu.VMEM((no, nz, mine, oc), jnp.bfloat16),
+            pltpu.VMEM((no, nz, mine, oc), jnp.float32),
+            pltpu.VMEM((no, nz, mine, oc), jnp.bfloat16),
+            pltpu.VMEM((nz - 1, no, mine, oc), jnp.bfloat16),
+            dma((no,)),
+            dma((ny - 1,)),
+            dma((ny - 1,)),
+            dma((nx - 1,)),
+            dma((nx - 1,)),
+            dma((no,)),
+            dma((no,)),
+            dma((nz - 1, no)),
+            dma((nz - 1, no)),
+        ],
+        compiler_params=pltpu.CompilerParams(
+            collective_id=1, has_side_effects=True, vmem_limit_bytes=48 * 1024 * 1024
+        ),
+        name="output",
+    )(attended, w_out)
+    return (branch.reshape(rows, steps, -1), new_keyvals)
+
+
+def on_device(*args):
+    hidden, _, w_query, w_keyval, w_out, cache_keys = args[:6]
+    nx, ny = lax.axis_size("gx"), lax.axis_size("gy")
+    local = cache_keys.shape[0] * hidden.shape[1]
+    fits = (
+        w_keyval.shape[2] == HD
+        and ny == KVH
+        and hidden.shape[1] == STEPS
+        and hidden.shape[0] * hidden.shape[1] % 16 == 0
+        and local == 4
+        and w_query.shape[1] % 256 == 0
+        and w_out.shape[1] % 512 == 0
+        and nx > 1
+    )
+    return with_kernels(*args) if fits else plain(*args)
+
+
 def solution(mesh):
     return jax.shard_map(
         on_device,

time: 248 us -> 88.6 us (0.36)
  Pallas kernels: 0 us -> 81.9 us
  blocking collectives: 76.4 us -> 0 us
  local copies, waits for them, and re-layouts: 72.8 us -> 4.75 us
  waiting for transfers between devices: 45.3 us -> 0 us
  matrix products: 27.2 us -> 0 us
  between operations: 14.2 us -> 0.73 us
  other arithmetic: 7.43 us -> 0.95 us
  starting transfers between devices: 3.64 us -> 0 us
    pallas_call x0 -> x3, Pallas kernels: none -> 81.9 us  [the longest x1 41.3 us: with_kernels(): pl.pallas_call(functools.partial(project_kernel, nx, ny), out_shape=jax.S...]
    psum x2 -> x0, blocking collectives: 57.8 us -> none  [the longest x1 46.4 us: on_device(): summed = lax.psum(partial_sums, 'gx')]
    unnamed x13 -> x8, local copies, waits for them, and re-layouts: 41.5 us -> 1.6 us
    reduce_scatter x1 -> x0, waiting for transfers between devices: 33.3 us -> none  [on_device(): lax.psum_scatter(product.reshape(lax.axis_size('gy') * out_rows_here, ste...]
    dot_general x8 -> x0, matrix products: 27.2 us -> none  [the longest x1 9.5 us: on_device(): jnp.dot(rows_all.reshape(lax.axis_size('gy') * out_rows_here * steps, hea...]
    reshape x5 -> x4, local copies, waits for them, and re-layouts: 18.3 us -> 3.05 us  [the longest x1 0.96 us: with_kernels(): hidden.reshape(mine, width)]
    all_to_all x4 -> x0, local copies, waits for them, and re-layouts: 12.1 us -> none  [the longest x3 12.1 us: on_device(): lax.all_to_all(attended, 'gy', split_axis=2, concat_axis=0, tiled=True)]
    all_to_all x1 -> x0, blocking collectives: 9.37 us -> none  [on_device(): lax.all_to_all(attended, 'gy', split_axis=2, concat_axis=0, tiled=True)]
  transfers between devices with their start and end apart: 3 -> 0, of which waited for: 3 -> 0; matrix products, arithmetic and copies ran while one was open for 7% -> 0% of each run, Pallas kernels for 0% -> 0%
where the time goes in v1:
time: 88.6 us; the launch traced here: 88.3 us
  Pallas kernels  81.9 us (92%)
  local copies, waits for them, and re-layouts  4.75 us (5%)
  other arithmetic  0.95 us (1%)
    pallas_call x1, Pallas kernels, with_kernels(): pl.pallas_call(functools.partial(project_kernel, nx, ny), out_shape=jax.S...  41.3 us
    pallas_call x1, Pallas kernels, with_kernels(): pl.pallas_call(functools.partial(output_kernel, nx, ny), out_shape=jax.Sh...  31.5 us
    pallas_call x1, Pallas kernels, with_kernels(): pl.pallas_call(attend_kernel, grid=(ny,), out_shape=(jax.ShapeDtypeStruct...  9.04 us

profile of v1, /device:TPU:0, one launch (start us, length us, event | category | flops | bytes accessed | tf_op | source)
XLA Modules:
  0.0 88.3 jit_solution(12991860501548965637)
XLA Ops:
  0.6 0.7 convert_element_type.6
  1.3 0.1 iota_add_fusion
  1.4 0.1 add.35
  1.5 0.1 fusion
  1.6 0.1 pad_maximum_fusion.2
  1.7 0.7 reshape.67.gain_ref
  2.4 1.0 %reshape.66.x_ref = bf16[16,4096]{1,0:T(8,128)(2,1)S(1)} reshape(bf16[8,2,4096]{2,1,0:T(2,128)(2,1)} %param.9) | data formatting | bytes 262144 | tf_op jit(solution)/shard_map/reshape | solution.py:545
  3.4 0.0 copy-start.2
  3.4 1.6 %copy-done.2 = bf16[2,4096,128]{2,1,0:T(8,128)(2,1)S(1)} copy-done((bf16[2,4096,128]{2,1,0:T(8,128)(2,1)S(1)}, bf16[2,4096,128]{2,1,0:T(8,128)(2,1)}, u32[]{:S(2)}) %copy-start.2) | copy-done | bytes 2097176
  5.0 0.0 copy-start
  5.0 0.0 copy-start.1
  5.0 0.0 copy-start.3
  5.0 41.3 %project.1.x_ref = bf16[8,80,128]{2,1,0:T(8,128)(2,1)S(1)} custom-call(bf16[16,4096]{1,0:T(8,128)(2,1)S(1)} %reshape.66.x_ref, bf16[1,4096]{1,0:T(2,128)(2,1)S(1)} %reshape.67.gain_ref, bf16[4096,2048]{1,0:T(8,128)(2,1)} %wq_hbm.1, bf16[2,4096,128]{2,1,0:T(8,128)(2,1)S(1)} %copy-done.2), custom_call_target="tpu_custom_call" | custom-call | tf_op jit(solution)/shard_map/project/pallas_call | solution.py:514
  46.4 0.0 copy-done
  46.4 0.0 copy-done.1
  46.4 0.0 copy-done.3
  46.4 9.0 %attend.1 = (bf16[8,64,128]{2,1,0:T(8,128)(2,1)S(1)}, f32[8,1024]{1,0:T(8,128)S(1)}) custom-call(s32[2]{0:T(128)S(1)} %copy-done.3, bf16[8,80,128]{2,1,0:T(8,128)(2,1)S(1)} %project.1.x_ref, f32[80,128]{1,0:T(8,128)S(1)} %pad_maximum_fusion.cos_ref, f32[80,128]{1,0:T(8,128)S(1)} %pad_maximum_fusion.1.sin_ref, bf16[2,1024,1024]{2,1,0:T(8,128)(2,1)S(1)} %copy-done, ...), custom_call_target="tpu_custom_call" | custom-call | tf_op jit(solution)/shard_map/attend/pallas_call | solution.py:556
  55.4 31.5 %output.1 = bf16[16,4096]{1,0:T(8,128)(2,1)S(1)} custom-call(bf16[8,64,128]{2,1,0:T(8,128)(2,1)S(1)} %get-tuple-element.4.att_ref, bf16[2048,4096]{1,0:T(8,128)(2,1)} %wo_hbm.1), custom_call_target="tpu_custom_call" | custom-call | tf_op jit(solution)/shard_map/output/pallas_call | solution.py:582
  87.0 0.8 reshape.72
  87.7 0.6 reshape.73
  (8 shorter events, 0.0 us)
Async XLA Ops:
  3.4 1.6 %copy-start.2 = (bf16[2,4096,128]{2,1,0:T(8,128)(2,1)S(1)}, bf16[2,4096,128]{2,1,0:T(8,128)(2,1)}, u32[]{:S(2)}) copy-start(bf16[2,4096,128]{2,1,0:T(8,128)(2,1)} %wkv_hbm.1) | copy-start | bytes 6291460
  5.0 41.4 %copy-start = (bf16[2,1024,1024]{2,1,0:T(8,128)(2,1)S(1)}, bf16[2,1024,1024]{2,1,0:T(8,128)(2,1)}, u32[]{:S(2)}) copy-start(bf16[2,1024,1024]{2,1,0:T(8,128)(2,1)} %key_ref.1) | copy-start | bytes 12582916
  5.0 41.4 %copy-start.1 = (bf16[2,1024,1024]{2,1,0:T(8,128)(2,1)S(1)}, bf16[2,1024,1024]{2,1,0:T(8,128)(2,1)}, u32[]{:S(2)}) copy-start(bf16[2,1024,1024]{2,1,0:T(8,128)(2,1)} %val_ref.1) | copy-start | bytes 12582916
  5.0 41.4 %copy-start.3 = (s32[2]{0:T(128)S(1)}, s32[2]{0:T(128)}, u32[]{:S(2)}) copy-start(s32[2]{0:T(128)} %len_ref.1) | copy-start | bytes 28

commit v2 on v1

--- a/solution.py
+++ b/solution.py
@@ -174,10 +174,13 @@
     pl.semaphore_wait(barrier, nx - 1 + ny - 1)
 
 
-def project_kernel(
-    nx, ny, x_ref, gain_ref, wq_hbm, wkv_hbm, out_ref,
+def layer_kernel(
+    nx, ny, x_ref, gain_ref, len_ref, cos_ref, sin_ref, wq_hbm, wkv_hbm, key_hbm, val_hbm, wo_hbm,
+    out_ref, kv_ref,
     wq, wkv, xbuf, sqbuf, parts, rbuf, qbuf, kvbuf, sendbuf, landed,
+    keys, vals, wo, att, abuf, fbuf, lbuf, prod, pbuf, qland, chip, zsend, zland,
     wq_sem, wkv_sem, sq_s, sq_r, g_s, g_r, rs_s, rs_r, a_s, a_r,
+    key_sem, val_sem, wo_sem, b_s, b_r, l_s, l_r, c_s, c_r, z_s, z_r,
 ):
     x = lax.axis_index("gx")
     y = lax.axis_index("gy")
@@ -188,6 +191,8 @@
     bc = wq.shape[2]
     head = wkv.shape[2]
     chunk = rbuf.shape[2]
+    no = wo.shape[0]
+    oc = wo.shape[2]
 
     def load_q(j):
         cols = pl.ds(j * bc, bc) if isinstance(j, int) else pl.ds(pl.multiple_of(j * bc, bc), bc)
@@ -257,6 +262,23 @@
 
     for zz in range(nz):
         hop(2 * zz + 1 - c, 2).wait_recv()
+
+    def load_cache(g):
+        cols = pl.ds(g * head, head) if isinstance(g, int) else pl.ds(pl.multiple_of(g * head, head), head)
+        return (
+            pltpu.make_async_copy(key_hbm.at[:, :, cols], keys.at[g], key_sem.at[g]),
+            pltpu.make_async_copy(val_hbm.at[:, :, cols], vals.at[g], val_sem.at[g]),
+        )
+
+    def load_o(j):
+        cols = pl.ds(j * oc, oc) if isinstance(j, int) else pl.ds(pl.multiple_of(j * oc, oc), oc)
+        return pltpu.make_async_copy(wo_hbm.at[:, cols], wo.at[j], wo_sem.at[j])
+
+    for g in range(ny):
+        for copy in load_cache(g):
+            copy.start()
+    for j in range(no):
+        load_o(j).start()
 
     def rs(j, d):
         to = lax.rem(x + d, nx)
@@ -314,9 +336,153 @@
     for d in range(1, ny):
         a2a(d).start()
     landed[y] = sendbuf[y]
+
+    def b2a(d):
+        to = lax.rem(y + d, ny)
+        return remote(att.at[to], abuf.at[y], b_s.at[d - 1], b_r.at[d - 1], "gy", to)
+
+    def one_head(g, q_block, key, val):
+        raw = q_block.astype(jnp.float32)
+        swapped = jnp.concatenate([raw[:, head // 2 :], raw[:, : head // 2]], axis=1)
+        turned = (raw * cos_ref[...] + swapped * sin_ref[...]).astype(jnp.bfloat16)
+        turned_f = turned.astype(jnp.float32)
+        slots = key.shape[1]
+        group = heads
+        count = STEPS * group
+        scale = HD ** (-0.5)
+        col = lax.broadcasted_iota(jnp.int32, (count, 4 * STEPS), 1)
+        step = lax.broadcasted_iota(jnp.int32, (count, 4 * STEPS), 0) // group
+        keep_new = (col % 4 == 0) & (col // 4 <= step)
+        slot = lax.broadcasted_iota(jnp.int32, (count, slots), 1)
+        keys_out, values_out, mixes = [], [], []
+        for b in range(key.shape[0]):
+            q = turned[b * count : (b + 1) * count]
+            base = key.shape[0] * count + b * 4 * STEPS
+            kv_turned = turned_f[base : base + 4 * STEPS]
+            kv_raw = raw[base : base + 4 * STEPS]
+            old = lax.dot_general(
+                q, key[b], (((1,), (1,)), ((), ())), preferred_element_type=jnp.float32
+            ) * scale
+            new = lax.dot_general(
+                q, kv_turned.astype(jnp.bfloat16), (((1,), (1,)), ((), ())),
+                preferred_element_type=jnp.float32,
+            ) * scale
+            old = jnp.where(slot < len_ref[b], old, -1e30)
+            new = jnp.where(keep_new, new, -1e30)
+            highest = jnp.maximum(
+                jnp.max(old, axis=-1, keepdims=True), jnp.max(new, axis=-1, keepdims=True)
+            )
+            old = jnp.exp(old - highest)
+            new = jnp.exp(new - highest)
+            denom = jnp.sum(old, axis=-1, keepdims=True) + jnp.sum(new, axis=-1, keepdims=True)
+            mixed = jnp.dot(old.astype(jnp.bfloat16), val[b], preferred_element_type=jnp.float32)
+            new = new.astype(jnp.bfloat16).astype(jnp.float32)
+            for r in range(STEPS):
+                mixed = mixed + new[:, 4 * r : 4 * r + 1] * kv_raw[4 * r + 1 : 4 * r + 2]
+                keys_out.append(kv_turned[4 * r : 4 * r + 1])
+                values_out.append(kv_raw[4 * r + 1 : 4 * r + 2])
+            mixes.append((mixed / denom).astype(jnp.bfloat16))
+        return jnp.concatenate(mixes, axis=0), jnp.concatenate(keys_out + values_out, axis=0)
+
+    def keep(g, mixed, fresh):
+        att[g] = mixed
+        kv_ref[:, pl.ds(pl.multiple_of(g * head, head), head)] = fresh
+
+    def two_heads(i, carry):
+        first = lax.rem(y + 1 + 2 * i, ny)
+        second = lax.rem(y + 2 + 2 * i, ny)
+        a2a(ny - 1 - 2 * i).wait_recv()
+
+        @pl.when(i < ny // 2 - 1)
+        def _():
+            a2a(ny - 2 - 2 * i).wait_recv()
+
+        for g in (first, second):
+            for copy in load_cache(g):
+                copy.wait()
+        loaded = [(g, landed[g], keys[g], vals[g]) for g in (first, second)]
+        results = [one_head(*items) for items in loaded]
+        keep(first, *results[0])
+        keep(second, *results[1])
+        b2a(2 * i + 1).start()
+
+        @pl.when(i < ny // 2 - 1)
+        def _():
+            b2a(2 * i + 2).start()
+
+        return carry
+
+    lax.fori_loop(0, ny // 2, two_heads, 0)
+    abuf[y] = att[y]
     for d in range(1, ny):
-        a2a(d).wait_recv()
-    out_ref[...] = landed[...]
+        b2a(d).wait_recv()
+    fbuf[...] = abuf[...].astype(jnp.float32).reshape(fbuf.shape)
+    for h in range(heads):
+        lbuf[x, :, h * head : (h + 1) * head] = fbuf[
+            pl.ds(h, chunk, stride=heads), :
+        ].astype(jnp.bfloat16)
+
+    def gather(d):
+        return remote(
+            lbuf.at[x], lbuf.at[x], l_s.at[d - 1], l_r.at[d - 1], "gx", lax.rem(x + d, nx)
+        )
+
+    for d in range(1, nx):
+        gather(d).start()
+    for d in range(1, nx):
+        gather(d).wait_recv()
+
+    def pair(j):
+        return remote(pbuf.at[j], qland.at[j], c_s.at[j], c_r.at[j], "gy", y + 1 - 2 * c)
+
+    def along(j, d):
+        to = lax.rem(z + d, nz)
+        return remote(
+            zsend.at[j, to], zland.at[d - 1, j], z_s.at[d - 1, j], z_r.at[d - 1, j], "gy", 2 * to + c
+        )
+
+    def pass_on(j):
+        pair(j).wait_recv()
+        chip[j] = prod[j, :, c] + qland[j].astype(jnp.float32)
+        zsend[j] = chip[j].astype(jnp.bfloat16)
+        for d in range(1, nz):
+            along(j, d).start()
+
+    def out_step(j, carry):
+        load_o(j).wait()
+        prod[j] = jnp.dot(
+            lbuf[...].reshape(nx * chunk, lbuf.shape[2]), wo[j], preferred_element_type=jnp.float32
+        ).reshape(prod.shape[1:])
+        pbuf[j] = prod[j, :, 1 - c].astype(jnp.bfloat16)
+        pair(j).start()
+
+        @pl.when(j > 0)
+        def _():
+            pass_on(j - 1)
+
+        return carry
+
+    lax.fori_loop(0, no, out_step, 0)
+    pass_on(no - 1)
+    for j in range(no):
+        total = chip[j, z]
+        for d in range(1, nz):
+            along(j, d).wait_recv()
+            total = total + zland[d - 1, j].astype(jnp.float32)
+        out_ref[:, j * oc : (j + 1) * oc] = total.astype(jnp.bfloat16)
+
+    for d in range(1, ny):
+        b2a(d).wait_send()
+    for d in range(1, nx):
+        gather(d).wait_send()
+
+    def done(j, carry):
+        pair(j).wait_send()
+        for d in range(1, nz):
+            along(j, d).wait_send()
+        return carry
+
+    lax.fori_loop(0, no, done, 0)
 
     for copy in sq_copies:
         copy.wait_send()
@@ -340,155 +506,6 @@
     lax.fori_loop(0, nblocks + 1, rs_done, 0)
     for d in range(1, ny):
         a2a(d).wait_send()
-
-
-def attend_kernel(len_ref, x_ref, cos_ref, sin_ref, key_ref, val_ref, out_ref, kv_ref):
-    rows = key_ref.shape[0]
-    slots = key_ref.shape[1]
-    head = key_ref.shape[2]
-    steps = STEPS
-    group = (x_ref.shape[1] // rows - 4 * steps) // steps
-    nq = steps * group
-    scale = HD ** (-0.5)
-    raw = x_ref[0].astype(jnp.float32)
-    swapped = jnp.concatenate([raw[:, head // 2 :], raw[:, : head // 2]], axis=1)
-    turned = (raw * cos_ref[...] + swapped * sin_ref[...]).astype(jnp.bfloat16)
-    turned_f = turned.astype(jnp.float32)
-    col = lax.broadcasted_iota(jnp.int32, (nq, 4 * steps), 1)
-    step = lax.broadcasted_iota(jnp.int32, (nq, 4 * steps), 0) // group
-    keep_new = (col % 4 == 0) & (col // 4 <= step)
-    slot = lax.broadcasted_iota(jnp.int32, (nq, slots), 1)
-    keys_out, values_out = [], []
-    for b in range(rows):
-        q = turned[b * nq : (b + 1) * nq]
-        base = rows * nq + b * 4 * steps
-        kv_turned = turned_f[base : base + 4 * steps]
-        kv_raw = raw[base : base + 4 * steps]
-        old = lax.dot_general(
-            q, key_ref[b], (((1,), (1,)), ((), ())), preferred_element_type=jnp.float32
-        ) * scale
-        new = lax.dot_general(
-            q, kv_turned.astype(jnp.bfloat16), (((1,), (1,)), ((), ())),
-            preferred_element_type=jnp.float32,
-        ) * scale
-        old = jnp.where(slot < len_ref[b], old, -1e30)
-        new = jnp.where(keep_new, new, -1e30)
-        highest = jnp.maximum(
-            jnp.max(old, axis=-1, keepdims=True), jnp.max(new, axis=-1, keepdims=True)
-        )
-        old = jnp.exp(old - highest)
-        new = jnp.exp(new - highest)
-        denom = jnp.sum(old, axis=-1, keepdims=True) + jnp.sum(new, axis=-1, keepdims=True)
-        mixed = jnp.dot(old.astype(jnp.bfloat16), val_ref[b], preferred_element_type=jnp.float32)
-        new = new.astype(jnp.bfloat16).astype(jnp.float32)
-        for r in range(steps):
-            mixed = mixed + new[:, 4 * r : 4 * r + 1] * kv_raw[4 * r + 1 : 4 * r + 2]
-            keys_out.append(kv_turned[4 * r : 4 * r + 1])
-            values_out.append(kv_raw[4 * r + 1 : 4 * r + 2])
-        out_ref[0, b * nq : (b + 1) * nq] = (mixed / denom).astype(jnp.bfloat16)
-    kv_ref[...] = jnp.concatenate(keys_out + values_out, axis=0)
-
-
-def output_kernel(
-    nx, ny, att_ref, wo_hbm, out_ref,
-    wo, abuf, fbuf, lbuf, prod, sbuf, rbuf, chip, zsend, zland,
-    wo_sem, a_s, a_r, g_s, g_r, c_s, c_r, z_s, z_r,
-):
-    x = lax.axis_index("gx")
-    y = lax.axis_index("gy")
-    nz = ny // 2
-    z = y // 2
-    c = lax.rem(y, 2)
-    nblocks = wo.shape[0]
-    bc = wo.shape[2]
-
-    def load(j):
-        cols = pl.ds(j * bc, bc) if isinstance(j, int) else pl.ds(pl.multiple_of(j * bc, bc), bc)
-        return pltpu.make_async_copy(wo_hbm.at[:, cols], wo.at[j], wo_sem.at[j])
-
-    for j in range(nblocks):
-        load(j).start()
-    greet(x, y, nx, ny)
-
-    def a2a(d):
-        to = lax.rem(y + d, ny)
-        return remote(att_ref.at[to], abuf.at[y], a_s.at[d - 1], a_r.at[d - 1], "gy", to)
-
-    for d in range(1, ny):
-        a2a(d).start()
-    abuf[y] = att_ref[y]
-    for d in range(1, ny):
-        a2a(d).wait_recv()
-    head = abuf.shape[2]
-    chunk = lbuf.shape[1]
-    heads = lbuf.shape[2] // head
-    fbuf[...] = abuf[...].astype(jnp.float32).reshape(fbuf.shape)
-    for h in range(heads):
-        lbuf[x, :, h * head : (h + 1) * head] = fbuf[
-            pl.ds(h, chunk, stride=heads), :
-        ].astype(jnp.bfloat16)
-
-    def gather(d):
-        return remote(
-            lbuf.at[x], lbuf.at[x], g_s.at[d - 1], g_r.at[d - 1], "gx", lax.rem(x + d, nx)
-        )
-
-    for d in range(1, nx):
-        gather(d).start()
-    for d in range(1, nx):
-        gather(d).wait_recv()
-
-    def pair(j):
-        return remote(sbuf.at[j], rbuf.at[j], c_s.at[j], c_r.at[j], "gy", y + 1 - 2 * c)
-
-    def along(j, d):
-        to = lax.rem(z + d, nz)
-        return remote(
-            zsend.at[j, to], zland.at[d - 1, j], z_s.at[d - 1, j], z_r.at[d - 1, j], "gy", 2 * to + c
-        )
-
-    def pass_on(j):
-        pair(j).wait_recv()
-        chip[j] = prod[j, :, c] + rbuf[j].astype(jnp.float32)
-        zsend[j] = chip[j].astype(jnp.bfloat16)
-        for d in range(1, nz):
-            along(j, d).start()
-
-    def block_step(j, carry):
-        load(j).wait()
-        prod[j] = jnp.dot(
-            lbuf[...].reshape(nx * chunk, lbuf.shape[2]), wo[j], preferred_element_type=jnp.float32
-        ).reshape(prod.shape[1:])
-        sbuf[j] = prod[j, :, 1 - c].astype(jnp.bfloat16)
-        pair(j).start()
-
-        @pl.when(j > 0)
-        def _():
-            pass_on(j - 1)
-
-        return carry
-
-    lax.fori_loop(0, nblocks, block_step, 0)
-    pass_on(nblocks - 1)
-    for j in range(nblocks):
-        total = chip[j, z]
-        for d in range(1, nz):
-            along(j, d).wait_recv()
-            total = total + zland[d - 1, j].astype(jnp.float32)
-        out_ref[:, j * bc : (j + 1) * bc] = total.astype(jnp.bfloat16)
-
-    for d in range(1, ny):
-        a2a(d).wait_send()
-    for d in range(1, nx):
-        gather(d).wait_send()
-
-    def done(j, carry):
-        pair(j).wait_send()
-        for d in range(1, nz):
-            along(j, d).wait_send()
-        return carry
-
-    lax.fori_loop(0, nblocks, done, 0)
 
 
 def with_kernels(
@@ -511,11 +528,25 @@
     vmem = pl.BlockSpec(memory_space=pltpu.VMEM)
     hbm = pl.BlockSpec(memory_space=pl.ANY)
     dma = pltpu.SemaphoreType.DMA
-    arrived = pl.pallas_call(
-        functools.partial(project_kernel, nx, ny),
-        out_shape=jax.ShapeDtypeStruct((ny, packed, HD), jnp.bfloat16),
-        in_specs=[vmem, vmem, hbm, hbm],
-        out_specs=vmem,
+    places = positions.astype(jnp.float32)[:, None] + jnp.arange(steps, dtype=jnp.float32)[None, :]
+    angles = places.reshape(local, 1) * rope_rates()[None, :]
+    cosine, sine = jnp.cos(angles), jnp.sin(angles)
+    cosine = jnp.concatenate([cosine, cosine], axis=-1)
+    sine = jnp.concatenate([-sine, sine], axis=-1)
+    spread = lambda table: jnp.concatenate(
+        [jnp.repeat(table, heads, axis=0), jnp.repeat(table, 4, axis=0)], axis=0
+    )
+    slots = cache_keys.shape[1]
+    oc = 512
+    no = w_out.shape[1] // oc
+    branch, new = pl.pallas_call(
+        functools.partial(layer_kernel, nx, ny),
+        out_shape=(
+            jax.ShapeDtypeStruct((mine, w_out.shape[1]), jnp.bfloat16),
+            jax.ShapeDtypeStruct((2 * local, KVH * HD), jnp.float32),
+        ),
+        in_specs=[vmem, vmem, pl.BlockSpec(memory_space=pltpu.SMEM), vmem, vmem] + [hbm] * 5,
+        out_specs=(vmem, vmem),
         scratch_shapes=[
             pltpu.VMEM((nq, width, bc), jnp.bfloat16),
             pltpu.VMEM(w_keyval.shape, jnp.bfloat16),
@@ -527,6 +558,19 @@
             pltpu.VMEM((chunk * 4, HD), jnp.float32),
             pltpu.VMEM((ny, packed, HD), jnp.bfloat16),
             pltpu.VMEM((ny, packed, HD), jnp.bfloat16),
+            pltpu.VMEM((ny, local_rows, slots, HD), jnp.bfloat16),
+            pltpu.VMEM((ny, local_rows, slots, HD), jnp.bfloat16),
+            pltpu.VMEM((no, cols, oc), jnp.bfloat16),
+            pltpu.VMEM((ny, local * heads, HD), jnp.bfloat16),
+            pltpu.VMEM((ny, local * heads, HD), jnp.bfloat16),
+            pltpu.VMEM((chunk * heads, HD), jnp.float32),
+            pltpu.VMEM((nx, chunk, cols), jnp.bfloat16),
+            pltpu.VMEM((no, nz, 2, mine, oc), jnp.float32),
+            pltpu.VMEM((no, nz, mine, oc), jnp.bfloat16),
+            pltpu.VMEM((no, nz, mine, oc), jnp.bfloat16),
+            pltpu.VMEM((no, nz, mine, oc), jnp.float32),
+            pltpu.VMEM((no, nz, mine, oc), jnp.bfloat16),
+            pltpu.VMEM((nz - 1, no, mine, oc), jnp.bfloat16),
             dma((nq,)),
             dma(()),
             dma((nx - 1,)),
@@ -537,64 +581,8 @@
             dma((nx - 1, nq + 1)),
             dma((ny - 1,)),
             dma((ny - 1,)),
-        ],
-        compiler_params=pltpu.CompilerParams(
-            collective_id=0, has_side_effects=True, vmem_limit_bytes=48 * 1024 * 1024
-        ),
-        name="project",
-    )(hidden.reshape(mine, width), norm_gain.reshape(1, width), w_query, w_keyval)
-
-    places = positions.astype(jnp.float32)[:, None] + jnp.arange(steps, dtype=jnp.float32)[None, :]
-    angles = places.reshape(local, 1) * rope_rates()[None, :]
-    cosine, sine = jnp.cos(angles), jnp.sin(angles)
-    cosine = jnp.concatenate([cosine, cosine], axis=-1)
-    sine = jnp.concatenate([-sine, sine], axis=-1)
-    spread = lambda table: jnp.concatenate(
-        [jnp.repeat(table, heads, axis=0), jnp.repeat(table, 4, axis=0)], axis=0
-    )
-    slots = cache_keys.shape[1]
-    attended, new = pl.pallas_call(
-        attend_kernel,
-        grid=(ny,),
-        out_shape=(
-            jax.ShapeDtypeStruct((ny, local * heads, HD), jnp.bfloat16),
-            jax.ShapeDtypeStruct((2 * local, KVH * HD), jnp.float32),
-        ),
-        in_specs=[
-            pl.BlockSpec(memory_space=pltpu.SMEM),
-            pl.BlockSpec((1, packed, HD), lambda g: (g, 0, 0)),
-            pl.BlockSpec((packed, HD), lambda g: (0, 0)),
-            pl.BlockSpec((packed, HD), lambda g: (0, 0)),
-            pl.BlockSpec((local_rows, slots, HD), lambda g: (0, 0, g)),
-            pl.BlockSpec((local_rows, slots, HD), lambda g: (0, 0, g)),
-        ],
-        out_specs=(
-            pl.BlockSpec((1, local * heads, HD), lambda g: (g, 0, 0)),
-            pl.BlockSpec((2 * local, HD), lambda g: (0, g)),
-        ),
-        compiler_params=pltpu.CompilerParams(vmem_limit_bytes=32 * 1024 * 1024),
-        name="attend",
-    )(cache_lengths, arrived, spread(cosine), spread(sine), cache_keys, cache_values)
-    new_keyvals = new.astype(jnp.bfloat16).reshape(2, local_rows, steps, KVH * HD)
-
-    oc = 512
-    no = w_out.shape[1] // oc
-    branch = pl.pallas_call(
-        functools.partial(output_kernel, nx, ny),
-        out_shape=jax.ShapeDtypeStruct((mine, w_out.shape[1]), jnp.bfloat16),
-        in_specs=[vmem, hbm],
-        out_specs=vmem,
-        scratch_shapes=[
-            pltpu.VMEM((no, cols, oc), jnp.bfloat16),
-            pltpu.VMEM((ny, local * heads, HD), jnp.bfloat16),
-            pltpu.VMEM((chunk * heads, HD), jnp.float32),
-            pltpu.VMEM((nx, chunk, cols), jnp.bfloat16),
-            pltpu.VMEM((no, nz, 2, mine, oc), jnp.float32),
-            pltpu.VMEM((no, nz, mine, oc), jnp.bfloat16),
-            pltpu.VMEM((no, nz, mine, oc), jnp.bfloat16),
-            pltpu.VMEM((no, nz, mine, oc), jnp.float32),
-            pltpu.VMEM((no, nz, mine, oc), jnp.bfloat16),
-            pltpu.VMEM((nz - 1, no, mine, oc), jnp.bfloat16),
+            dma((ny,)),
+            dma((ny,)),
             dma((no,)),
             dma((ny - 1,)),
             dma((ny - 1,)),
@@ -606,10 +594,14 @@
             dma((nz - 1, no)),
         ],
         compiler_params=pltpu.CompilerParams(
-            collective_id=1, has_side_effects=True, vmem_limit_bytes=48 * 1024 * 1024
+            collective_id=0, has_side_effects=True, vmem_limit_bytes=60 * 1024 * 1024
         ),
-        name="output",
-    )(attended, w_out)
+        name="layer",
+    )(
+        hidden.reshape(mine, width), norm_gain.reshape(1, width), cache_lengths,
+        spread(cosine), spread(sine), w_query, w_keyval, cache_keys, cache_values, w_out,
+    )
+    new_keyvals = new.astype(jnp.bfloat16).reshape(2, local_rows, steps, KVH * HD)
     return (branch.reshape(rows, steps, -1), new_keyvals)
 
 

time: 88.6 us -> 84.6 us (0.955)
  Pallas kernels: 81.9 us -> 75.4 us
  other arithmetic: 0.95 us -> 2.94 us
    pallas_call x3 -> x1, Pallas kernels: 81.9 us -> 75.4 us  [with_kernels(): pl.pallas_call(functools.partial(layer_kernel, nx, ny), out_shape=(jax.Sh...]
    unnamed x8 -> x0, local copies, waits for them, and re-layouts: 1.6 us -> none
    concatenate x2, other arithmetic: 0.01 us -> 1.24 us  [with_kernels(): jnp.concatenate([jnp.repeat(table, heads, axis=0), jnp.repeat(table, 4, a...]
    reshape x1, local copies, waits for them, and re-layouts: 0.76 us -> 1.67 us  [with_kernels(): return (branch.reshape(rows, steps, -1), new_keyvals)]
where the time goes in v2:
time: 84.6 us; the launch traced here: 84.3 us
  Pallas kernels  75.4 us (89%)
  local copies, waits for them, and re-layouts  5.31 us (6%)
  other arithmetic  2.94 us (3%)
    pallas_call x1, Pallas kernels, with_kernels(): pl.pallas_call(functools.partial(layer_kernel, nx, ny), out_shape=(jax.Sh...  75.4 us

profile of v2, /device:TPU:0, one launch (start us, length us, event | category | flops | bytes accessed | tf_op | source)
XLA Modules:
  0.0 84.3 jit_solution(9073140974962539470)
XLA Ops:
  0.6 0.7 convert_element_type.6
  1.3 0.1 iota_add_fusion
  1.4 0.1 add.35
  1.5 0.1 fusion
  1.6 0.1 pad_maximum_fusion.2
  1.7 1.3 %reshape.67.gain_ref = bf16[1,4096]{1,0:T(2,128)(2,1)} reshape(bf16[4096]{0:T(1024)(128)(2,1)} %param.10) | data formatting | bytes 16384 | tf_op jit(solution)/shard_map/reshape | solution.py:601
  3.0 0.6 pad_maximum_fusion.1.sin_ref
  3.6 0.6 pad_maximum_fusion.cos_ref
  4.2 1.6 %reshape.66.x_ref = bf16[16,4096]{1,0:T(8,128)(2,1)} reshape(bf16[8,2,4096]{2,1,0:T(2,128)(2,1)} %param.9) | data formatting | bytes 262144 | tf_op jit(solution)/shard_map/reshape | solution.py:601
  5.8 75.4 %layer.1 = (bf16[16,4096]{1,0:T(8,128)(2,1)}, f32[8,1024]{1,0:T(8,128)}) custom-call(bf16[16,4096]{1,0:T(8,128)(2,1)} %reshape.66.x_ref, bf16[1,4096]{1,0:T(2,128)(2,1)} %reshape.67.gain_ref, s32[2]{0:T(128)} %len_ref.1, f32[80,128]{1,0:T(8,128)} %pad_maximum_fusion.cos_ref, f32[80,128]{1,0:T(8,128)} %pad_maximum_fusion.1.sin_ref, ...), custom_call_target="tpu_custom_call" | custom-call | tf_op jit(solution)/shard_map/layer/pallas_call | solution.py:542
  81.3 1.7 %reshape.72 = bf16[8,2,4096]{2,1,0:T(2,128)(2,1)} reshape(bf16[16,4096]{1,0:T(8,128)(2,1)} %get-tuple-element.4) | data formatting | bytes 262144 | tf_op jit(solution)/shard_map/reshape | solution.py:605
  82.9 0.8 convert_element_type.7
  83.7 0.6 reshape.73
  (5 shorter events, 0.0 us)

commit v3 on v2

--- a/solution.py
+++ b/solution.py
@@ -177,7 +177,7 @@
 def layer_kernel(
     nx, ny, x_ref, gain_ref, len_ref, cos_ref, sin_ref, wq_hbm, wkv_hbm, key_hbm, val_hbm, wo_hbm,
     out_ref, kv_ref,
-    wq, wkv, xbuf, sqbuf, parts, rbuf, qbuf, kvbuf, sendbuf, landed,
+    xf, cosbuf, sinbuf, wq, wkv, xbuf, sqbuf, parts, rbuf, qbuf, kvbuf, sendbuf, landed,
     keys, vals, wo, att, abuf, fbuf, lbuf, prod, pbuf, qland, chip, zsend, zland,
     wq_sem, wkv_sem, sq_s, sq_r, g_s, g_r, rs_s, rs_r, a_s, a_r,
     key_sem, val_sem, wo_sem, b_s, b_r, l_s, l_r, c_s, c_r, z_s, z_r,
@@ -205,7 +205,10 @@
     for j in range(nblocks):
         load_q(j).start()
 
-    features = x_ref[...].astype(jnp.float32)
+    count = x_ref.shape[1]
+    for i in range(x_ref.shape[0]):
+        xf[count * i : count * (i + 1), :] = x_ref[i].astype(jnp.float32)
+    features = xf[...]
     squares = jnp.sum(features * features, axis=-1, keepdims=True)
     sqbuf[0] = jnp.broadcast_to(squares, sqbuf.shape[1:])
     greet(x, y, nx, ny)
@@ -221,47 +224,63 @@
     for d in range(1, nx):
         total = total + sqbuf[d]
     inverse = lax.rsqrt(total[:, :1] / D + norm_epsilon)
-    xbuf[y] = (features * inverse * gain_ref[...].astype(jnp.float32)).astype(jnp.bfloat16)
-
-    def hop(block, k):
+    normed = (
+        features * inverse * gain_ref[...].astype(jnp.float32).reshape(1, features.shape[1])
+    ).astype(jnp.bfloat16)
+    half = xbuf.shape[3]
+    for t in range(2):
+        xbuf[t, y] = normed[:, t * half : (t + 1) * half]
+
+    def hop(t, block, k):
         dest = (y - 2, y + 2, y + 1 - 2 * c)[k]
-        return remote(xbuf.at[block], xbuf.at[block], g_s.at[block, k], g_r.at[block], "gy", dest)
-
-    @pl.when(z > 0)
-    def _():
-        hop(y, 0).start()
-
-    @pl.when(z < nz - 1)
-    def _():
-        hop(y, 1).start()
-
-    hop(y, 2).start()
-    for d in range(1, nz):
-
+        return remote(
+            xbuf.at[t, block], xbuf.at[t, block], g_s.at[t, block, k], g_r.at[t, block], "gy", dest
+        )
+
+    def begin(t):
+        @pl.when(z > 0)
+        def _():
+            hop(t, y, 0).start()
+
+        @pl.when(z < nz - 1)
+        def _():
+            hop(t, y, 1).start()
+
+        hop(t, y, 2).start()
+
+    def forward(t, d):
         @pl.when(z - d >= 0)
         def _():
             block = y - 2 * d
-            hop(block, 2).wait_recv()
+            hop(t, block, 2).wait_recv()
 
             @pl.when(z < nz - 1)
             def _():
-                hop(block, 1).start()
-
-            hop(block, 2).start()
+                hop(t, block, 1).start()
+
+            hop(t, block, 2).start()
 
         @pl.when(z + d < nz)
         def _():
             block = y + 2 * d
-            hop(block, 2).wait_recv()
+            hop(t, block, 2).wait_recv()
 
             @pl.when(z > 0)
             def _():
-                hop(block, 0).start()
-
-            hop(block, 2).start()
-
-    for zz in range(nz):
-        hop(2 * zz + 1 - c, 2).wait_recv()
+                hop(t, block, 0).start()
+
+            hop(t, block, 2).start()
+
+    def from_pair(t):
+        for zz in range(nz):
+            hop(t, 2 * zz + 1 - c, 2).wait_recv()
+
+    begin(0)
+    for d in range(1, nz):
+        forward(0, d)
+        if d == 1:
+            begin(1)
+    from_pair(0)
 
     def load_cache(g):
         cols = pl.ds(g * head, head) if isinstance(g, int) else pl.ds(pl.multiple_of(g * head, head), head)
@@ -287,25 +306,41 @@
             parts.at[j, rows, :], rbuf.at[d - 1, j], rs_s.at[d - 1, j], rs_r.at[d - 1, j], "gx", to
         )
 
-    tokens = xbuf.shape[0] * xbuf.shape[1]
+    tokens = xbuf.shape[1] * xbuf.shape[2]
+
+    def times(t, weights):
+        return jnp.dot(
+            xbuf[t].reshape(tokens, half), weights, preferred_element_type=jnp.float32
+        )
+
+    def first_half(j, carry):
+        load_q(j).wait()
+        parts[j] = times(0, wq[j, :half])
+        return carry
+
     load_kv().wait()
     for n in range(2):
-        parts[nblocks, :, n * head : (n + 1) * head] = jnp.dot(
-            xbuf[...].reshape(tokens, xbuf.shape[2]), wkv[n], preferred_element_type=jnp.float32
-        )
+        parts[nblocks, :, n * head : (n + 1) * head] = times(0, wkv[n, :half])
+    done = 0
+    for d in range(1, nz):
+        upto = nblocks * d // nz
+        lax.fori_loop(done, upto, first_half, 0)
+        forward(1, d)
+        done = upto
+    lax.fori_loop(done, nblocks, first_half, 0)
+    from_pair(1)
+    for n in range(2):
+        parts[nblocks, :, n * head : (n + 1) * head] += times(1, wkv[n, half:])
     for d in range(1, nx):
         rs(nblocks, d).start()
 
-    def block_step(j, carry):
-        load_q(j).wait()
-        parts[j] = jnp.dot(
-            xbuf[...].reshape(tokens, xbuf.shape[2]), wq[j], preferred_element_type=jnp.float32
-        )
+    def second_half(j, carry):
+        parts[j] += times(1, wq[j, half:])
         for d in range(1, nx):
             rs(j, d).start()
         return carry
 
-    lax.fori_loop(0, nblocks, block_step, 0)
+    lax.fori_loop(0, nblocks, second_half, 0)
 
     own = pl.ds(pl.multiple_of(x * chunk, chunk), chunk)
     per_block = bc // head
@@ -337,6 +372,18 @@
         a2a(d).start()
     landed[y] = sendbuf[y]
 
+    for buf, first, last in ((cosbuf, 1.0, 1.0), (sinbuf, -1.0, 1.0)):
+        table = cos_ref if buf is cosbuf else sin_ref
+        lines = []
+        for b in range(table.shape[0]):
+            line = table[b]
+            line = jnp.concatenate([line * first, line * last], axis=1)
+            lines += [line[r : r + 1] for r in range(STEPS)]
+        for r, line in enumerate(lines):
+            buf[r * heads : (r + 1) * heads, :] = jnp.broadcast_to(line, (heads, head))
+        tail = [jnp.broadcast_to(line, (4, head)) for line in lines]
+        buf[local * heads :, :] = jnp.concatenate(tail, axis=0)
+
     def b2a(d):
         to = lax.rem(y + d, ny)
         return remote(att.at[to], abuf.at[y], b_s.at[d - 1], b_r.at[d - 1], "gy", to)
@@ -344,7 +391,7 @@
     def one_head(g, q_block, key, val):
         raw = q_block.astype(jnp.float32)
         swapped = jnp.concatenate([raw[:, head // 2 :], raw[:, : head // 2]], axis=1)
-        turned = (raw * cos_ref[...] + swapped * sin_ref[...]).astype(jnp.bfloat16)
+        turned = (raw * cosbuf[...] + swapped * sinbuf[...]).astype(jnp.bfloat16)
         turned_f = turned.astype(jnp.float32)
         slots = key.shape[1]
         group = heads
@@ -379,14 +426,17 @@
             new = new.astype(jnp.bfloat16).astype(jnp.float32)
             for r in range(STEPS):
                 mixed = mixed + new[:, 4 * r : 4 * r + 1] * kv_raw[4 * r + 1 : 4 * r + 2]
-                keys_out.append(kv_turned[4 * r : 4 * r + 1])
-                values_out.append(kv_raw[4 * r + 1 : 4 * r + 2])
+            for out, block, at in ((keys_out, kv_turned, 0), (values_out, kv_raw, 1)):
+                lines = [block[4 * r + at : 4 * r + at + 1] for r in range(STEPS)]
+                out.append(jnp.concatenate(lines, axis=0).astype(jnp.bfloat16))
             mixes.append((mixed / denom).astype(jnp.bfloat16))
-        return jnp.concatenate(mixes, axis=0), jnp.concatenate(keys_out + values_out, axis=0)
+        return jnp.concatenate(mixes, axis=0), (keys_out, values_out)
 
     def keep(g, mixed, fresh):
         att[g] = mixed
-        kv_ref[:, pl.ds(pl.multiple_of(g * head, head), head)] = fresh
+        for n in range(2):
+            for b in range(kv_ref.shape[1]):
+                kv_ref[n, b, :, pl.ds(pl.multiple_of(g * head, head), head)] = fresh[n][b]
 
     def two_heads(i, carry):
         first = lax.rem(y + 1 + 2 * i, ny)
@@ -417,20 +467,39 @@
     for d in range(1, ny):
         b2a(d).wait_recv()
     fbuf[...] = abuf[...].astype(jnp.float32).reshape(fbuf.shape)
-    for h in range(heads):
-        lbuf[x, :, h * head : (h + 1) * head] = fbuf[
-            pl.ds(h, chunk, stride=heads), :
-        ].astype(jnp.bfloat16)
-
-    def gather(d):
+
+    def gather(t, d):
         return remote(
-            lbuf.at[x], lbuf.at[x], l_s.at[d - 1], l_r.at[d - 1], "gx", lax.rem(x + d, nx)
+            lbuf.at[t, x], lbuf.at[t, x], l_s.at[t, d - 1], l_r.at[t, d - 1], "gx", lax.rem(x + d, nx)
         )
 
+    kept = heads // 2
+    for t in range(2):
+        for h in range(kept):
+            lbuf[t, x, :, h * head : (h + 1) * head] = fbuf[
+                pl.ds(t * kept + h, chunk, stride=heads), :
+            ].astype(jnp.bfloat16)
+        for d in range(1, nx):
+            gather(t, d).start()
+
+    def out_times(t, j):
+        depth = kept * head
+        return jnp.dot(
+            lbuf[t].reshape(nx * chunk, depth), wo[j, t * depth : (t + 1) * depth],
+            preferred_element_type=jnp.float32,
+        ).reshape(prod.shape[1:])
+
     for d in range(1, nx):
-        gather(d).start()
+        gather(0, d).wait_recv()
+
+    def out_first(j, carry):
+        load_o(j).wait()
+        prod[j] = out_times(0, j)
+        return carry
+
+    lax.fori_loop(0, no, out_first, 0)
     for d in range(1, nx):
-        gather(d).wait_recv()
+        gather(1, d).wait_recv()
 
     def pair(j):
         return remote(pbuf.at[j], qland.at[j], c_s.at[j], c_r.at[j], "gy", y + 1 - 2 * c)
@@ -449,10 +518,7 @@
             along(j, d).start()
 
     def out_step(j, carry):
-        load_o(j).wait()
-        prod[j] = jnp.dot(
-            lbuf[...].reshape(nx * chunk, lbuf.shape[2]), wo[j], preferred_element_type=jnp.float32
-        ).reshape(prod.shape[1:])
+        prod[j] += out_times(1, j)
         pbuf[j] = prod[j, :, 1 - c].astype(jnp.bfloat16)
         pair(j).start()
 
@@ -469,12 +535,16 @@
         for d in range(1, nz):
             along(j, d).wait_recv()
             total = total + zland[d - 1, j].astype(jnp.float32)
-        out_ref[:, j * oc : (j + 1) * oc] = total.astype(jnp.bfloat16)
+        for i in range(out_ref.shape[0]):
+            out_ref[i, :, j * oc : (j + 1) * oc] = total[count * i : count * (i + 1)].astype(
+                jnp.bfloat16
+            )
 
     for d in range(1, ny):
         b2a(d).wait_send()
-    for d in range(1, nx):
-        gather(d).wait_send()
+    for t in range(2):
+        for d in range(1, nx):
+            gather(t, d).wait_send()
 
     def done(j, carry):
         pair(j).wait_send()
@@ -486,17 +556,18 @@
 
     for copy in sq_copies:
         copy.wait_send()
-    for zz in range(nz):
-        block = 2 * zz + c
-        hop(block, 2).wait_send()
-
-        @pl.when((zz >= z) & (z > 0))
-        def _():
-            hop(block, 0).wait_send()
-
-        @pl.when((zz <= z) & (z < nz - 1))
-        def _():
-            hop(block, 1).wait_send()
+    for t in range(2):
+        for zz in range(nz):
+            block = 2 * zz + c
+            hop(t, block, 2).wait_send()
+
+            @pl.when((zz >= z) & (z > 0))
+            def _():
+                hop(t, block, 0).wait_send()
+
+            @pl.when((zz <= z) & (z < nz - 1))
+            def _():
+                hop(t, block, 1).wait_send()
 
     def rs_done(j, carry):
         for d in range(1, nx):
@@ -529,28 +600,25 @@
     hbm = pl.BlockSpec(memory_space=pl.ANY)
     dma = pltpu.SemaphoreType.DMA
     places = positions.astype(jnp.float32)[:, None] + jnp.arange(steps, dtype=jnp.float32)[None, :]
-    angles = places.reshape(local, 1) * rope_rates()[None, :]
-    cosine, sine = jnp.cos(angles), jnp.sin(angles)
-    cosine = jnp.concatenate([cosine, cosine], axis=-1)
-    sine = jnp.concatenate([-sine, sine], axis=-1)
-    spread = lambda table: jnp.concatenate(
-        [jnp.repeat(table, heads, axis=0), jnp.repeat(table, 4, axis=0)], axis=0
-    )
+    angles = places[..., None] * rope_rates()
     slots = cache_keys.shape[1]
     oc = 512
     no = w_out.shape[1] // oc
-    branch, new = pl.pallas_call(
+    return pl.pallas_call(
         functools.partial(layer_kernel, nx, ny),
         out_shape=(
-            jax.ShapeDtypeStruct((mine, w_out.shape[1]), jnp.bfloat16),
-            jax.ShapeDtypeStruct((2 * local, KVH * HD), jnp.float32),
+            jax.ShapeDtypeStruct((rows, steps, w_out.shape[1]), jnp.bfloat16),
+            jax.ShapeDtypeStruct((2, local_rows, steps, KVH * HD), jnp.bfloat16),
         ),
         in_specs=[vmem, vmem, pl.BlockSpec(memory_space=pltpu.SMEM), vmem, vmem] + [hbm] * 5,
         out_specs=(vmem, vmem),
         scratch_shapes=[
+            pltpu.VMEM((mine, width), jnp.float32),
+            pltpu.VMEM((packed, HD), jnp.float32),
+            pltpu.VMEM((packed, HD), jnp.float32),
             pltpu.VMEM((nq, width, bc), jnp.bfloat16),
             pltpu.VMEM(w_keyval.shape, jnp.bfloat16),
-            pltpu.VMEM((ny, mine, width), jnp.bfloat16),
+            pltpu.VMEM((2, ny, mine, width // 2), jnp.bfloat16),
             pltpu.VMEM((nx, mine, 128), jnp.float32),
             pltpu.VMEM((nq + 1, tokens, bc), jnp.float32),
             pltpu.VMEM((nx - 1, nq + 1, chunk, bc), jnp.float32),
@@ -564,7 +632,7 @@
             pltpu.VMEM((ny, local * heads, HD), jnp.bfloat16),
             pltpu.VMEM((ny, local * heads, HD), jnp.bfloat16),
             pltpu.VMEM((chunk * heads, HD), jnp.float32),
-            pltpu.VMEM((nx, chunk, cols), jnp.bfloat16),
+            pltpu.VMEM((2, nx, chunk, cols // 2), jnp.bfloat16),
             pltpu.VMEM((no, nz, 2, mine, oc), jnp.float32),
             pltpu.VMEM((no, nz, mine, oc), jnp.bfloat16),
             pltpu.VMEM((no, nz, mine, oc), jnp.bfloat16),
@@ -575,8 +643,8 @@
             dma(()),
             dma((nx - 1,)),
             dma((nx - 1,)),
-            dma((ny, 3)),
-            dma((ny,)),
+            dma((2, ny, 3)),
+            dma((2, ny)),
             dma((nx - 1, nq + 1)),
             dma((nx - 1, nq + 1)),
             dma((ny - 1,)),
@@ -586,8 +654,8 @@
             dma((no,)),
             dma((ny - 1,)),
             dma((ny - 1,)),
-            dma((nx - 1,)),
-            dma((nx - 1,)),
+            dma((2, nx - 1)),
+            dma((2, nx - 1)),
             dma((no,)),
             dma((no,)),
             dma((nz - 1, no)),
@@ -598,11 +666,9 @@
         ),
         name="layer",
     )(
-        hidden.reshape(mine, width), norm_gain.reshape(1, width), cache_lengths,
-        spread(cosine), spread(sine), w_query, w_keyval, cache_keys, cache_values, w_out,
-    )
-    new_keyvals = new.astype(jnp.bfloat16).reshape(2, local_rows, steps, KVH * HD)
-    return (branch.reshape(rows, steps, -1), new_keyvals)
+        hidden, norm_gain, cache_lengths, jnp.cos(angles), jnp.sin(angles),
+        w_query, w_keyval, cache_keys, cache_values, w_out,
+    )
 
 
 def on_device(*args):

time: 84.6 us -> 85.5 us (1.011)
  Pallas kernels: 75.4 us -> 80.1 us
  local copies, waits for them, and re-layouts: 5.31 us -> 2.99 us
  other arithmetic: 2.94 us -> 1.46 us
    reshape x4 -> x0, local copies, waits for them, and re-layouts: 5.22 us -> none  [the longest x1 1.67 us: with_kernels(): return (branch.reshape(rows, steps, -1), new_keyvals)]
    pallas_call x1, Pallas kernels: 75.4 us -> 80.1 us  [with_kernels(): pl.pallas_call(functools.partial(layer_kernel, nx, ny), out_shape=(jax.Sh...]
    unnamed x0 -> x2, local copies, waits for them, and re-layouts: none -> 2.99 us
    concatenate x3 -> x0, other arithmetic: 1.32 us -> none  [the longest x2 1.24 us: with_kernels(): jnp.concatenate([jnp.repeat(table, heads, axis=0), jnp.repeat(table, 4, a...]
where the time goes in v3:
time: 85.5 us; the launch traced here: 85.2 us
  Pallas kernels  80.1 us (94%)
  local copies, waits for them, and re-layouts  2.99 us (3%)
  other arithmetic  1.46 us (2%)
    pallas_call x1, Pallas kernels, with_kernels(): pl.pallas_call(functools.partial(layer_kernel, nx, ny), out_shape=(jax.Sh...  80.1 us
    unnamed x2, local copies, waits for them, and re-layouts  2.99 us

profile of v3, /device:TPU:0, one launch (start us, length us, event | category | flops | bytes accessed | tf_op | source)
XLA Modules:
  0.0 85.2 jit_solution(11639217402289225209)
XLA Ops:
  0.6 0.7 convert_element_type.3
  1.3 0.1 iota_add_fusion
  1.4 0.7 multiply_sine_fusion
  2.1 80.1 %layer.1 = (bf16[8,2,4096]{2,1,0:T(2,128)(2,1)}, bf16[2,2,2,1024]{3,2,1,0:T(2,128)(2,1)}) custom-call(bf16[8,2,4096]{2,1,0:T(2,128)(2,1)} %x_ref.1, bf16[4096]{0:T(1024)(128)(2,1)} %gain_ref.1, s32[2]{0:T(128)} %len_ref.1, f32[2,2,64]{2,1,0:T(2,128)} %get-tuple-element.3.cos_ref, f32[2,2,64]{2,1,0:T(2,128)} %get-tuple-element.2.sin_ref, ...), custom_call_target="tpu_custom_call" | custom-call | tf_op jit(solution)/shard_map/layer/pallas_call | solution.py:607
  82.2 1.7 %copy.13 = bf16[8,2,4096]{2,1,0:T(2,128)(2,1)} copy(bf16[8,2,4096]{2,1,0:T(2,128)(2,1)} %get-tuple-element.6) | data formatting | bytes 262144
  83.9 1.3 %copy.14 = bf16[2,2,2,1024]{3,2,1,0:T(2,128)(2,1)} copy(bf16[2,2,2,1024]{3,2,1,0:T(2,128)(2,1)} %get-tuple-element.7) | data formatting | bytes 32768
  (1 shorter events, 0.0 us)

commit v4 on v3

--- a/solution.py
+++ b/solution.py
@@ -228,8 +228,7 @@
         features * inverse * gain_ref[...].astype(jnp.float32).reshape(1, features.shape[1])
     ).astype(jnp.bfloat16)
     half = xbuf.shape[3]
-    for t in range(2):
-        xbuf[t, y] = normed[:, t * half : (t + 1) * half]
+    xbuf[0, y] = normed
 
     def hop(t, block, k):
         dest = (y - 2, y + 2, y + 1 - 2 * c)[k]
@@ -278,8 +277,6 @@
     begin(0)
     for d in range(1, nz):
         forward(0, d)
-        if d == 1:
-            begin(1)
     from_pair(0)
 
     def load_cache(g):
@@ -293,12 +290,6 @@
         cols = pl.ds(j * oc, oc) if isinstance(j, int) else pl.ds(pl.multiple_of(j * oc, oc), oc)
         return pltpu.make_async_copy(wo_hbm.at[:, cols], wo.at[j], wo_sem.at[j])
 
-    for g in range(ny):
-        for copy in load_cache(g):
-            copy.start()
-    for j in range(no):
-        load_o(j).start()
-
     def rs(j, d):
         to = lax.rem(x + d, nx)
         rows = pl.ds(pl.multiple_of(to * chunk, chunk), chunk)
@@ -313,34 +304,22 @@
             xbuf[t].reshape(tokens, half), weights, preferred_element_type=jnp.float32
         )
 
-    def first_half(j, carry):
-        load_q(j).wait()
-        parts[j] = times(0, wq[j, :half])
-        return carry
-
     load_kv().wait()
     for n in range(2):
-        parts[nblocks, :, n * head : (n + 1) * head] = times(0, wkv[n, :half])
-    done = 0
-    for d in range(1, nz):
-        upto = nblocks * d // nz
-        lax.fori_loop(done, upto, first_half, 0)
-        forward(1, d)
-        done = upto
-    lax.fori_loop(done, nblocks, first_half, 0)
-    from_pair(1)
-    for n in range(2):
-        parts[nblocks, :, n * head : (n + 1) * head] += times(1, wkv[n, half:])
+        parts[nblocks, :, n * head : (n + 1) * head] = times(0, wkv[n])
     for d in range(1, nx):
         rs(nblocks, d).start()
 
-    def second_half(j, carry):
-        parts[j] += times(1, wq[j, half:])
+    def block_step(j, carry):
+        load_q(j).wait()
+        parts[j] = times(0, wq[j])
         for d in range(1, nx):
             rs(j, d).start()
+        for copy in load_cache(j):
+            copy.start()
         return carry
 
-    lax.fori_loop(0, nblocks, second_half, 0)
+    lax.fori_loop(0, nblocks, block_step, 0)
 
     own = pl.ds(pl.multiple_of(x * chunk, chunk), chunk)
     per_block = bc // head
@@ -460,8 +439,11 @@
         def _():
             b2a(2 * i + 2).start()
 
+        for n in range(per_turn):
+            load_o(per_turn * i + n).start()
         return carry
 
+    per_turn = no // (ny // 2)
     lax.fori_loop(0, ny // 2, two_heads, 0)
     abuf[y] = att[y]
     for d in range(1, ny):
@@ -473,33 +455,14 @@
             lbuf.at[t, x], lbuf.at[t, x], l_s.at[t, d - 1], l_r.at[t, d - 1], "gx", lax.rem(x + d, nx)
         )
 
-    kept = heads // 2
-    for t in range(2):
-        for h in range(kept):
-            lbuf[t, x, :, h * head : (h + 1) * head] = fbuf[
-                pl.ds(t * kept + h, chunk, stride=heads), :
-            ].astype(jnp.bfloat16)
-        for d in range(1, nx):
-            gather(t, d).start()
-
-    def out_times(t, j):
-        depth = kept * head
-        return jnp.dot(
-            lbuf[t].reshape(nx * chunk, depth), wo[j, t * depth : (t + 1) * depth],
-            preferred_element_type=jnp.float32,
-        ).reshape(prod.shape[1:])
-
+    for h in range(heads):
+        lbuf[0, x, :, h * head : (h + 1) * head] = fbuf[
+            pl.ds(h, chunk, stride=heads), :
+        ].astype(jnp.bfloat16)
+    for d in range(1, nx):
+        gather(0, d).start()
     for d in range(1, nx):
         gather(0, d).wait_recv()
-
-    def out_first(j, carry):
-        load_o(j).wait()
-        prod[j] = out_times(0, j)
-        return carry
-
-    lax.fori_loop(0, no, out_first, 0)
-    for d in range(1, nx):
-        gather(1, d).wait_recv()
 
     def pair(j):
         return remote(pbuf.at[j], qland.at[j], c_s.at[j], c_r.at[j], "gy", y + 1 - 2 * c)
@@ -518,7 +481,10 @@
             along(j, d).start()
 
     def out_step(j, carry):
-        prod[j] += out_times(1, j)
+        load_o(j).wait()
+        prod[j] = jnp.dot(
+            lbuf[0].reshape(nx * chunk, lbuf.shape[3]), wo[j], preferred_element_type=jnp.float32
+        ).reshape(prod.shape[1:])
         pbuf[j] = prod[j, :, 1 - c].astype(jnp.bfloat16)
         pair(j).start()
 
@@ -542,9 +508,8 @@
 
     for d in range(1, ny):
         b2a(d).wait_send()
-    for t in range(2):
-        for d in range(1, nx):
-            gather(t, d).wait_send()
+    for d in range(1, nx):
+        gather(0, d).wait_send()
 
     def done(j, carry):
         pair(j).wait_send()
@@ -556,7 +521,7 @@
 
     for copy in sq_copies:
         copy.wait_send()
-    for t in range(2):
+    for t in range(1):
         for zz in range(nz):
             block = 2 * zz + c
             hop(t, block, 2).wait_send()
@@ -577,6 +542,11 @@
     lax.fori_loop(0, nblocks + 1, rs_done, 0)
     for d in range(1, ny):
         a2a(d).wait_send()
+
+
+def write_kernel(branch_ref, kv_ref, branch_out, kv_out):
+    branch_out[...] = branch_ref[...]
+    kv_out[...] = kv_ref[...]
 
 
 def with_kernels(
@@ -604,7 +574,7 @@
     slots = cache_keys.shape[1]
     oc = 512
     no = w_out.shape[1] // oc
-    return pl.pallas_call(
+    made = pl.pallas_call(
         functools.partial(layer_kernel, nx, ny),
         out_shape=(
             jax.ShapeDtypeStruct((rows, steps, w_out.shape[1]), jnp.bfloat16),
@@ -618,7 +588,7 @@
             pltpu.VMEM((packed, HD), jnp.float32),
             pltpu.VMEM((nq, width, bc), jnp.bfloat16),
             pltpu.VMEM(w_keyval.shape, jnp.bfloat16),
-            pltpu.VMEM((2, ny, mine, width // 2), jnp.bfloat16),
+            pltpu.VMEM((1, ny, mine, width), jnp.bfloat16),
             pltpu.VMEM((nx, mine, 128), jnp.float32),
             pltpu.VMEM((nq + 1, tokens, bc), jnp.float32),
             pltpu.VMEM((nx - 1, nq + 1, chunk, bc), jnp.float32),
@@ -632,7 +602,7 @@
             pltpu.VMEM((ny, local * heads, HD), jnp.bfloat16),
             pltpu.VMEM((ny, local * heads, HD), jnp.bfloat16),
             pltpu.VMEM((chunk * heads, HD), jnp.float32),
-            pltpu.VMEM((2, nx, chunk, cols // 2), jnp.bfloat16),
+            pltpu.VMEM((1, nx, chunk, cols), jnp.bfloat16),
             pltpu.VMEM((no, nz, 2, mine, oc), jnp.float32),
             pltpu.VMEM((no, nz, mine, oc), jnp.bfloat16),
             pltpu.VMEM((no, nz, mine, oc), jnp.bfloat16),
@@ -643,8 +613,8 @@
             dma(()),
             dma((nx - 1,)),
             dma((nx - 1,)),
-            dma((2, ny, 3)),
-            dma((2, ny)),
+            dma((1, ny, 3)),
+            dma((1, ny)),
             dma((nx - 1, nq + 1)),
             dma((nx - 1, nq + 1)),
             dma((ny - 1,)),
@@ -654,8 +624,8 @@
             dma((no,)),
             dma((ny - 1,)),
             dma((ny - 1,)),
-            dma((2, nx - 1)),
-            dma((2, nx - 1)),
+            dma((1, nx - 1)),
+            dma((1, nx - 1)),
             dma((no,)),
             dma((no,)),
             dma((nz - 1, no)),
@@ -669,6 +639,13 @@
         hidden, norm_gain, cache_lengths, jnp.cos(angles), jnp.sin(angles),
         w_query, w_keyval, cache_keys, cache_values, w_out,
     )
+    return pl.pallas_call(
+        write_kernel,
+        out_shape=tuple(jax.ShapeDtypeStruct(item.shape, item.dtype) for item in made),
+        in_specs=[vmem, vmem],
+        out_specs=(vmem, vmem),
+        name="write",
+    )(*made)
 
 
 def on_device(*args):
@@ -684,6 +661,8 @@
         and w_query.shape[1] % 256 == 0
         and w_out.shape[1] % 512 == 0
         and nx > 1
+        and w_query.shape[1] // 256 == ny
+        and (w_out.shape[1] // 512) % (ny // 2) == 0
     )
     return with_kernels(*args) if fits else plain(*args)
 

time: 85.5 us -> 79.4 us (0.929)
  Pallas kernels: 80.1 us -> 77.1 us
  local copies, waits for them, and re-layouts: 2.99 us -> 0 us
    pallas_call x1, Pallas kernels: 80.1 us -> 75.5 us  [with_kernels(): pl.pallas_call(functools.partial(layer_kernel, nx, ny), out_shape=(jax.Sh...]
    unnamed x2 -> x0, local copies, waits for them, and re-layouts: 2.99 us -> none
    pallas_call x0 -> x1, Pallas kernels: none -> 1.57 us  [with_kernels(): pl.pallas_call(write_kernel, out_shape=tuple((jax.ShapeDtypeStruct(item.s...]
where the time goes in v4:
time: 79.4 us; the launch traced here: 79.2 us
  Pallas kernels  77.1 us (97%)
  other arithmetic  1.46 us (2%)
    pallas_call x1, Pallas kernels, with_kernels(): pl.pallas_call(functools.partial(layer_kernel, nx, ny), out_shape=(jax.Sh...  75.5 us

profile of v4, /device:TPU:0, one launch (start us, length us, event | category | flops | bytes accessed | tf_op | source)
XLA Modules:
  0.0 79.2 jit_solution(10087822953672741055)
XLA Ops:
  0.6 0.7 convert_element_type.3
  1.3 0.1 iota_add_fusion
  1.4 0.7 multiply_sine_fusion
  2.1 75.5 %layer.1 = (bf16[8,2,4096]{2,1,0:T(2,128)(2,1)}, bf16[2,2,2,1024]{3,2,1,0:T(2,128)(2,1)}) custom-call(bf16[8,2,4096]{2,1,0:T(2,128)(2,1)} %x_ref.1, bf16[4096]{0:T(1024)(128)(2,1)} %gain_ref.1, s32[2]{0:T(128)} %len_ref.1, f32[2,2,64]{2,1,0:T(2,128)} %get-tuple-element.7.cos_ref, f32[2,2,64]{2,1,0:T(2,128)} %get-tuple-element.6.sin_ref, ...), custom_call_target="tpu_custom_call" | custom-call | tf_op jit(solution)/shard_map/layer/pallas_call | solution.py:577
  77.6 1.6 %write.1 = (bf16[8,2,4096]{2,1,0:T(2,128)(2,1)}, bf16[2,2,2,1024]{3,2,1,0:T(2,128)(2,1)}) custom-call(bf16[8,2,4096]{2,1,0:T(2,128)(2,1)} %get-tuple-element.4.branch_ref, bf16[2,2,2,1024]{3,2,1,0:T(2,128)(2,1)} %get-tuple-element.5.kv_ref), custom_call_target="tpu_custom_call" | custom-call | tf_op jit(solution)/shard_map/write/pallas_call | solution.py:642
  (1 shorter events, 0.0 us)

commit v5 on v4

--- a/solution.py
+++ b/solution.py
@@ -227,14 +227,13 @@
     normed = (
         features * inverse * gain_ref[...].astype(jnp.float32).reshape(1, features.shape[1])
     ).astype(jnp.bfloat16)
-    half = xbuf.shape[3]
+    half = xbuf.shape[3] // 2
     xbuf[0, y] = normed
 
     def hop(t, block, k):
         dest = (y - 2, y + 2, y + 1 - 2 * c)[k]
-        return remote(
-            xbuf.at[t, block], xbuf.at[t, block], g_s.at[t, block, k], g_r.at[t, block], "gy", dest
-        )
+        piece = xbuf.at[0, block, :, pl.ds(t * half, half)]
+        return remote(piece, piece, g_s.at[t, block, k], g_r.at[t, block], "gy", dest)
 
     def begin(t):
         @pl.when(z > 0)
@@ -274,10 +273,13 @@
         for zz in range(nz):
             hop(t, 2 * zz + 1 - c, 2).wait_recv()
 
-    begin(0)
+    for t in range(2):
+        begin(t)
     for d in range(1, nz):
-        forward(0, d)
-    from_pair(0)
+        for t in range(2):
+            forward(t, d)
+    for t in range(2):
+        from_pair(t)
 
     def load_cache(g):
         cols = pl.ds(g * head, head) if isinstance(g, int) else pl.ds(pl.multiple_of(g * head, head), head)
@@ -301,7 +303,7 @@
 
     def times(t, weights):
         return jnp.dot(
-            xbuf[t].reshape(tokens, half), weights, preferred_element_type=jnp.float32
+            xbuf[t].reshape(tokens, xbuf.shape[3]), weights, preferred_element_type=jnp.float32
         )
 
     load_kv().wait()
@@ -417,34 +419,37 @@
             for b in range(kv_ref.shape[1]):
                 kv_ref[n, b, :, pl.ds(pl.multiple_of(g * head, head), head)] = fresh[n][b]
 
-    def two_heads(i, carry):
-        first = lax.rem(y + 1 + 2 * i, ny)
-        second = lax.rem(y + 2 + 2 * i, ny)
-        a2a(ny - 1 - 2 * i).wait_recv()
-
-        @pl.when(i < ny // 2 - 1)
+    turns = ny // 4
+    per_turn = no // turns
+
+    def four_heads(i, carry):
+        each = [lax.rem(y + 1 + 4 * i + n, ny) for n in range(4)]
+        for n in range(3):
+            a2a(ny - 1 - 4 * i - n).wait_recv()
+
+        @pl.when(i < turns - 1)
         def _():
-            a2a(ny - 2 - 2 * i).wait_recv()
-
-        for g in (first, second):
+            a2a(ny - 4 - 4 * i).wait_recv()
+
+        for g in each:
             for copy in load_cache(g):
                 copy.wait()
-        loaded = [(g, landed[g], keys[g], vals[g]) for g in (first, second)]
+        loaded = [(g, landed[g], keys[g], vals[g]) for g in each]
         results = [one_head(*items) for items in loaded]
-        keep(first, *results[0])
-        keep(second, *results[1])
-        b2a(2 * i + 1).start()
-
-        @pl.when(i < ny // 2 - 1)
+        for g, result in zip(each, results):
+            keep(g, *result)
+        for n in range(3):
+            b2a(4 * i + n + 1).start()
+
+        @pl.when(i < turns - 1)
         def _():
-            b2a(2 * i + 2).start()
+            b2a(4 * i + 4).start()
 
         for n in range(per_turn):
             load_o(per_turn * i + n).start()
         return carry
 
-    per_turn = no // (ny // 2)
-    lax.fori_loop(0, ny // 2, two_heads, 0)
+    lax.fori_loop(0, turns, four_heads, 0)
     abuf[y] = att[y]
     for d in range(1, ny):
         b2a(d).wait_recv()
@@ -521,7 +526,7 @@
 
     for copy in sq_copies:
         copy.wait_send()
-    for t in range(1):
+    for t in range(2):
         for zz in range(nz):
             block = 2 * zz + c
             hop(t, block, 2).wait_send()
@@ -613,8 +618,8 @@
             dma(()),
             dma((nx - 1,)),
             dma((nx - 1,)),
-            dma((1, ny, 3)),
-            dma((1, ny)),
+            dma((2, ny, 3)),
+            dma((2, ny)),
             dma((nx - 1, nq + 1)),
             dma((nx - 1, nq + 1)),
             dma((ny - 1,)),
@@ -662,7 +667,7 @@
         and w_out.shape[1] % 512 == 0
         and nx > 1
         and w_query.shape[1] // 256 == ny
-        and (w_out.shape[1] // 512) % (ny // 2) == 0
+        and (w_out.shape[1] // 512) % (ny // 4) == 0
     )
     return with_kernels(*args) if fits else plain(*args)
 

time: 79.4 us -> 78.9 us (level)
  no operation moved by 1% of the time
where the time goes in v5:
time: 78.9 us; the launch traced here: 78.7 us
  Pallas kernels  76.6 us (97%)
  other arithmetic  1.46 us (2%)
    pallas_call x1, Pallas kernels, with_kernels(): pl.pallas_call(functools.partial(layer_kernel, nx, ny), out_shape=(jax.Sh...  75 us

profile of v5, /device:TPU:0, one launch (start us, length us, event | category | flops | bytes accessed | tf_op | source)
XLA Modules:
  0.0 78.7 jit_solution(9540231457841100266)
XLA Ops:
  0.6 0.7 convert_element_type.3
  1.3 0.1 iota_add_fusion
  1.4 0.7 multiply_sine_fusion
  2.1 75.0 %layer.1 = (bf16[8,2,4096]{2,1,0:T(2,128)(2,1)}, bf16[2,2,2,1024]{3,2,1,0:T(2,128)(2,1)}) custom-call(bf16[8,2,4096]{2,1,0:T(2,128)(2,1)} %x_ref.1, bf16[4096]{0:T(1024)(128)(2,1)} %gain_ref.1, s32[2]{0:T(128)} %len_ref.1, f32[2,2,64]{2,1,0:T(2,128)} %get-tuple-element.7.cos_ref, f32[2,2,64]{2,1,0:T(2,128)} %get-tuple-element.6.sin_ref, ...), custom_call_target="tpu_custom_call" | custom-call | tf_op jit(solution)/shard_map/layer/pallas_call | solution.py:582
  77.1 1.6 %write.1 = (bf16[8,2,4096]{2,1,0:T(2,128)(2,1)}, bf16[2,2,2,1024]{3,2,1,0:T(2,128)(2,1)}) custom-call(bf16[8,2,4096]{2,1,0:T(2,128)(2,1)} %get-tuple-element.4.branch_ref, bf16[2,2,2,1024]{3,2,1,0:T(2,128)(2,1)} %get-tuple-element.5.kv_ref), custom_call_target="tpu_custom_call" | custom-call | tf_op jit(solution)/shard_map/write/pallas_call | solution.py:647
  (1 shorter events, 0.0 us)
